TPU v7x, 256 devices: a whole 4x4x8 slice. The times are simulated.
256 devices in a mesh: foot: 32 (over z, x_lo, core), layer: 8 (over x_hi, y).
Axes of the slice: x: 4 (x_hi: 2, x_lo: 2; x = x_hi * 2 + x_lo), y: 4, z: 8, core: 2. Of those that a mesh axis runs over, the one named last changes fastest.
Arguments:
- conserved: float32 [5, 4, 4, 4, 64, 8192], P(None, None, None, None, 'layer', 'foot'), as said below
- register: float32 [5, 4, 4, 4, 64, 8192], P(None, None, None, None, 'layer', 'foot'), may hold values from -3 to 3
- neighbour: int32 [4, 8192], P(None, 'foot'), may hold values from 0 to 8191, as said below
- side_type: int32 [4, 8192], P(None, 'foot'), may hold values from 0 to 2, as said below
Outputs:
- advanced: float32 [5, 4, 4, 4, 64, 8192], P(None, None, None, None, 'layer', 'foot')
- new_register: float32 [5, 4, 4, 4, 64, 8192], P(None, None, None, None, 'layer', 'foot')
Inputs may be any that keep to these rules, and one draw needn't show every extreme that they name: `conserved`: every density lies in 0.5 to 1.5, every pressure in 0.4 to 1.6, every velocity component within -0.8 to 0.8. `neighbour`: where side_type is 2 the entry names the column itself; elsewhere the named column's side s xor 1 names this column back, and the two elements share their face nodes index for index. The footprint is a grid of 8 x 4 square tiles of 16 x 16 columns; the columns of tile (a, b) are the 256 columns c with c // 256 = 4 * a + b, in any order. A side 0 or 1 of a column names a column of tile (a - 1, b) or (a + 1, b) or of its own tile, a side 2 or 3 one of tile (a, b - 1) or (a, b + 1) or of its own tile; sides on the district's outer edge have side_type 2. `side_type`: A side of type 1 faces a side of type 1.
All inputs are finite; a program needn't handle non-finite values.
Results may differ from a plain program's by a relative error of at most 0.0003.
Values sent between devices are 32-bit elements; how exact they have to be, the bound alone decides.
A program may use at most 128 MiB of HBM per device.

v0:
```python
import jax
import jax.numpy as jnp
import numpy as np
from jax import lax
from jax.sharding import PartitionSpec as P

ADIABATIC = 1.4
LIFT_FACTOR = 6.0
TIME_STEP = 0.02
SECTION_DECAY = -0.4178904745
SECTION_WEIGHT = 1.720146321549
FREE_STREAM = (1.0, 0.3, 0.1, 0.0, 1.0 / 0.56 + 0.05)


def extended(array, sides, width):
    for axis, dim in sides:
        size, length = (lax.axis_size(axis), array.shape[dim])
        up = [(i, (i + 1) % size) for i in range(size - 1)]
        down = [(j, i) for i, j in up]
        last = lax.slice_in_dim(array, length - width, length, axis=dim)
        leading = lax.slice_in_dim(array, 0, width, axis=dim)
        before = lax.ppermute(last, axis, up)
        after = lax.ppermute(leading, axis, down)
        array = jnp.concatenate([before, array, after], axis=dim)
    return array


def from_behind(array, axis, by):
    length = lax.axis_size(axis)
    pairs = [(i, i + by) for i in range(length) if 0 <= i + by < length]
    return lax.ppermute(array, axis, pairs)


def derivative_entries():
    nodes = np.array([-1.0, -1.0 / np.sqrt(5.0), 1.0 / np.sqrt(5.0), 1.0])
    products = np.array(
        [
            np.prod(
                [
                    nodes[target_node] - nodes[another]
                    for another in range(4)
                    if another != target_node
                ]
            )
            for target_node in range(4)
        ]
    )
    matrix = np.zeros((4, 4))
    for target_node in range(4):
        for source_node in range(4):
            if target_node != source_node:
                matrix[target_node, source_node] = (
                    products[target_node]
                    / products[source_node]
                    / (nodes[target_node] - nodes[source_node])
                )
            else:
                matrix[target_node, target_node] = sum(
                    (
                        1.0 / (nodes[target_node] - nodes[another])
                        for another in range(4)
                        if another != target_node
                    )
                )
    return np.asarray(matrix, dtype=np.float32)


def primitives(conserved):
    density = conserved[0]
    velocity = conserved[1:4] / density
    pressure = (ADIABATIC - 1.0) * (
        conserved[4] - 0.5 * density * jnp.sum(velocity * velocity, axis=0)
    )
    return (density, velocity, pressure)


def normal_flux(conserved, direction, velocity, pressure):
    normal_velocity = velocity[direction]
    entries = [conserved[1 + direction]]
    for component in range(3):
        entry_value = conserved[1 + component] * normal_velocity
        if component == direction:
            entry_value = entry_value + pressure
        entries.append(entry_value)
    entries.append((conserved[4] + pressure) * normal_velocity)
    return jnp.stack(entries)


def face_term(inside, outside, direction, orientation):
    density_in, velocity_in, pressure_in = primitives(inside)
    density_out, velocity_out, pressure_out = primitives(outside)
    flux_in = orientation * normal_flux(inside, direction, velocity_in, pressure_in)
    flux_out = orientation * normal_flux(outside, direction, velocity_out, pressure_out)
    speed_in = jnp.abs(velocity_in[direction]) + jnp.sqrt(ADIABATIC * pressure_in / density_in)
    speed_out = jnp.abs(velocity_out[direction]) + jnp.sqrt(ADIABATIC * pressure_out / density_out)
    wave_speed = jnp.maximum(speed_in, speed_out)
    common = 0.5 * (flux_in + flux_out) - 0.5 * wave_speed * (outside - inside)
    return -LIFT_FACTOR * (common - flux_in)


def mirrored(inside, direction):
    reflect = jnp.where(jnp.arange(5) == 1 + direction, -1.0, 1.0).astype(jnp.float32)
    return inside * reflect.reshape((5,) + (1,) * (inside.ndim - 1))


def far_state(inside):
    stream = jnp.asarray(FREE_STREAM, dtype=jnp.float32).reshape((5,) + (1,) * (inside.ndim - 1))
    return jnp.broadcast_to(stream, inside.shape)


def outer_state(inside, ghost_side, face_kind, direction):
    return jnp.where(
        face_kind == 0,
        ghost_side,
        jnp.where(face_kind == 1, mirrored(inside, direction), far_state(inside)),
    )


def node_slice(field, axis_number, node):
    return lax.index_in_dim(field, node, axis_number, keepdims=False)


def apply_derivative(field, axis_number, entries):
    results = []
    for target_node in range(4):
        total = float(entries[target_node, 0]) * node_slice(field, axis_number, 0)
        for source_node in range(1, 4):
            total = total + float(entries[target_node, source_node]) * node_slice(
                field, axis_number, source_node
            )
        results.append(total)
    return jnp.stack(results, axis=axis_number)


def tendency(conserved, outsides):
    density, velocity, pressure = primitives(conserved)
    entries = derivative_entries()
    volume = apply_derivative(normal_flux(conserved, 0, velocity, pressure), 1, entries)
    volume = volume + apply_derivative(normal_flux(conserved, 1, velocity, pressure), 2, entries)
    volume = volume + apply_derivative(normal_flux(conserved, 2, velocity, pressure), 3, entries)
    change = -volume
    change = change.at[:, 0].add(face_term(conserved[:, 0], outsides[0], 0, -1.0))
    change = change.at[:, 3].add(face_term(conserved[:, 3], outsides[1], 0, 1.0))
    change = change.at[:, :, 0].add(face_term(conserved[:, :, 0], outsides[2], 1, -1.0))
    change = change.at[:, :, 3].add(face_term(conserved[:, :, 3], outsides[3], 1, 1.0))
    change = change.at[:, :, :, 0].add(face_term(conserved[:, :, :, 0], outsides[4], 2, -1.0))
    change = change.at[:, :, :, 3].add(face_term(conserved[:, :, :, 3], outsides[5], 2, 1.0))
    return change


def select_rows(source, selector):
    return jnp.dot(
        source, selector, precision=lax.Precision.HIGHEST, preferred_element_type=jnp.float32
    )


def per_device(conserved, register, neighbour, side_type):
    layers = conserved.shape[4]
    columns = conserved.shape[5]
    bottoms = conserved[:, :, :, 0]
    tops = conserved[:, :, :, 3]
    rim_traces = jnp.stack([bottoms[:, :, :, 0], tops[:, :, :, layers - 1]], axis=3)
    padded = extended(rim_traces, (("layer", 3),), 1)
    layer_index = lax.axis_index("layer")
    layer_total = lax.axis_size("layer")
    below_ghost = jnp.where(layer_index == 0, mirrored(bottoms[:, :, :, 0], 2), padded[:, :, :, 0])
    above_ghost = jnp.where(
        layer_index == layer_total - 1, far_state(tops[:, :, :, 0]), padded[:, :, :, 3]
    )
    outside_low = jnp.concatenate([below_ghost[:, :, :, None], tops[:, :, :, : layers - 1]], axis=3)
    outside_high = jnp.concatenate([bottoms[:, :, :, 1:], above_ghost[:, :, :, None]], axis=3)
    lateral = [conserved[:, 0], conserved[:, 3], conserved[:, :, 0], conserved[:, :, 3]]
    flat_sides = [lateral_face.reshape(80 * layers, columns) for lateral_face in lateral]
    self_index = lax.axis_index("foot")
    target_device = neighbour // columns
    local_column = neighbour % columns
    remote = target_device != self_index
    column_steps = jnp.arange(columns, dtype=jnp.int32)
    outsides = []
    for facing in range(4):
        column_here = local_column[facing]
        remote_here = remote[facing]
        hits = column_steps[:, None] == column_here[None, :]
        local_select = (hits & jnp.logical_not(remote_here)[None, :]).astype(jnp.float32)
        ghost_flat = select_rows(flat_sides[facing ^ 1], local_select)
        arrived = from_behind(flat_sides[facing ^ 1], "foot", (4, -4, 1, -1)[facing])
        remote_select = (hits & remote_here[None, :]).astype(jnp.float32)
        ghost_flat = ghost_flat + select_rows(arrived, remote_select)
        ghost_side = ghost_flat.reshape(5, 4, 4, layers, columns)
        outsides.append(outer_state(lateral[facing], ghost_side, side_type[facing], facing // 2))
    outsides.append(outside_low)
    outsides.append(outside_high)
    change = tendency(conserved, outsides)
    register_next = SECTION_DECAY * register + TIME_STEP * change
    return (conserved + SECTION_WEIGHT * register_next, register_next)


def solution(mesh):
    return jax.shard_map(
        per_device,
        mesh=mesh,
        in_specs=(
            P(None, None, None, None, "layer", "foot"),
            P(None, None, None, None, "layer", "foot"),
            P(None, "foot"),
            P(None, "foot"),
        ),
        out_specs=(
            P(None, None, None, None, "layer", "foot"),
            P(None, None, None, None, "layer", "foot"),
        ),
        check_vma=False,
    )
```

profile of v0, /device:TPU:123, one launch (start us, length us, event | category | flops | bytes accessed | tf_op | source)
XLA Modules:
  0.0 136.1 jit_solution(7869228209686661601)
XLA Ops:
  0.6 2.1 %slice.825 = f32[5,1,4,4,8,256]{5,4,3,2,1,0:T(8,128)} slice(f32[5,4,4,4,8,256]{5,4,3,2,1,0:T(8,128)} %param.21), slice={[0:5], [0:1], [0:4], [0:4], [0:8], [0:256]} | slice | bytes 1310720 | tf_op jit(solution)/shard_map/slice | solution.py:142
  2.8 1.9 %collective-permute-start.1 = (f32[640,256]{1,0:T(8,128)}, f32[640,256]{1,0:T(8,128)}, u32[]{:S(2)}, u32[]{:S(2)}) collective-permute-start(f32[640,256]{1,0:T(8,128)} %bitcast.42), channel_id=1, source_target_pairs={{32,0},{40,8},{48,16},{56,24},{64,32},{72,40},{80,48},{88,56},{96,... | collective-permute-start | bytes 1966088 | tf_op jit(solution)/shard_map/ppermute | solution.py:31
  4.7 2.3 %slice_bitcast_fusion.9 = (f32[5,4,4,8,256]{4,3,2,1,0:T(8,128)}, f32[5,1,4,4,8,256]{5,4,3,2,0,1:T(8,128)}) fusion(f32[5,4,4,4,8,256]{5,4,3,2,1,0:T(8,128)} %param.21), kind=kLoop, calls=%fused_computation.483 | loop fusion | bytes 1966080 | tf_op jit(solution)/shard_map/squeeze | solution.py:143
  7.0 4.7 %collective-permute-start = (f32[640,256]{1,0:T(8,128)}, f32[640,256]{1,0:T(8,128)}, u32[]{:S(2)}, u32[]{:S(2)}) collective-permute-start(f32[640,256]{1,0:T(8,128)} %bitcast.15), channel_id=1, source_target_pairs={{0,32},{8,40},{16,48},{24,56},{32,64},{40,72},{48,80},{56,88},{64,... | collective-permute-start | bytes 1966088 | tf_op jit(solution)/shard_map/ppermute | solution.py:31
  13.0 2.9 %collective-permute-start.3 = (f32[640,256]{1,0:T(8,128)}, f32[640,256]{1,0:T(8,128)}, u32[]{:S(2)}, u32[]{:S(2)}) collective-permute-start(f32[640,256]{1,0:T(8,128)} %bitcast.94), channel_id=1, source_target_pairs={{8,0},{16,8},{24,16},{32,24},{40,32},{48,40},{56,48},{64,56},{72,6... | collective-permute-start | bytes 1966088 | tf_op jit(solution)/shard_map/ppermute | solution.py:31
  15.9 4.7 %collective-permute-start.2 = (f32[640,256]{1,0:T(8,128)}, f32[640,256]{1,0:T(8,128)}, u32[]{:S(2)}, u32[]{:S(2)}) collective-permute-start(f32[640,256]{1,0:T(8,128)} %bitcast.68), channel_id=1, source_target_pairs={{0,8},{8,16},{16,24},{24,32},{32,40},{40,48},{48,56},{56,64},{64,7... | collective-permute-start | bytes 1966088 | tf_op jit(solution)/shard_map/ppermute | solution.py:31
  20.8 3.4 %collective-permute-start.4 = (f32[5,4,4,1,256]{4,3,1,2,0:T(1,128)S(1)}, f32[5,4,4,1,256]{4,3,1,2,0:T(1,128)}, u32[]{:S(2)}, u32[]{:S(2)}) collective-permute-start(f32[5,4,4,1,256]{4,3,1,2,0:T(1,128)S(1)} %slice.999), channel_id=1, source_target_pairs={{0,1},{1,2},{2,3},{3,4},{4,5},{5,6},{6,7},{8,9},{9,10},{10,11},{11... | collective-permute-start | bytes 245768 | tf_op jit(solution)/shard_map/ppermute | solution.py:22
  37.3 2.1 %copy.362 = f32[5,4,4,4,8,256]{5,4,3,2,0,1:T(8,128)} copy(f32[5,4,4,4,8,256]{5,4,2,0,1,3:T(8,128)S(1)} %fusion) | data formatting | bytes 5242880 | tf_op jit(solution)/shard_map/neg | solution.py:141
  58.2 2.2 %fusion.228 = (f32[5,4,4,7,256]{4,3,2,0,1:T(8,128)S(1)}, f32[5,4,4,1,7,256]{5,4,2,0,1,3:T(8,128)}) fusion(f32[5,4,4,8,256]{4,3,2,0,1:T(8,128)} %slice_bitcast_fusion), kind=kLoop, calls=%fused_computation.493 | loop fusion | bytes 1720320 | tf_op jit(solution)/shard_map/slice | solution.py:171
  65.8 1.8 %fusion.80 = f32[256,640]{1,0:T(8,128)S(1)} fusion(f32[640,256]{1,0:T(8,128)} %bitcast.42, s32[256]{0:T(256)S(1)} %bitcast.818, pred[256]{0:T(512)(128)(4,1)S(1)} %copy-done.98), kind=kOutput, calls=%fused_computation.261 | convolution fusion | flops 503513088 | bytes 1312000 | tf_op jit(solution)/shard_map/dot_general | solution.py:152
  67.6 2.7 %fusion.83 = f32[256,640]{1,0:T(8,128)} fusion(f32[640,256]{1,0:T(8,128)} %bitcast.15, s32[256]{0:T(256)S(1)} %bitcast.816, pred[256]{0:T(512)(128)(4,1)S(1)} %copy-done.97), kind=kOutput, calls=%fused_computation.262 | convolution fusion | flops 503513088 | bytes 1312000 | tf_op jit(solution)/shard_map/dot_general | solution.py:152
  72.3 2.6 %fusion.74 = f32[256,640]{1,0:T(8,128)} fusion(f32[640,256]{1,0:T(8,128)} %bitcast.94, s32[256]{0:T(256)S(1)} %bitcast.814, pred[256]{0:T(512)(128)(4,1)S(1)} %copy-done.96), kind=kOutput, calls=%fused_computation.259 | convolution fusion | flops 503513088 | bytes 1312000 | tf_op jit(solution)/shard_map/dot_general | solution.py:152
  74.9 2.6 %fusion.77 = f32[256,640]{1,0:T(8,128)} fusion(f32[640,256]{1,0:T(8,128)} %bitcast.68, s32[256]{0:T(256)S(1)} %bitcast.812, pred[256]{0:T(512)(128)(4,1)S(1)} %get-tuple-element.91), kind=kOutput, calls=%fused_computation.260 | convolution fusion | flops 503513088 | bytes 1312000 | tf_op jit(solution)/shard_map/dot_general | solution.py:152
  81.4 2.1 %collective-permute-start.5 = (f32[5,4,4,1,256]{4,3,1,2,0:T(1,128)S(1)}, f32[5,4,4,1,256]{4,3,1,2,0:T(1,128)S(1)}, u32[]{:S(2)}, u32[]{:S(2)}) collective-permute-start(f32[5,4,4,1,256]{4,3,1,2,0:T(1,128)S(1)} %get-tuple-element.210), channel_id=1, source_target_pairs={{1,0},{2,1},{3,2},{4,3},{5,4},{6,5},{7,6},{9,8},{10,9},{11,10},{12... | collective-permute-start | bytes 245768 | tf_op jit(solution)/shard_map/ppermute | solution.py:23
  83.7 6.6 %collective-permute-done.5 = f32[5,4,4,1,256]{4,3,1,2,0:T(1,128)S(1)} collective-permute-done((f32[5,4,4,1,256]{4,3,1,2,0:T(1,128)S(1)}, f32[5,4,4,1,256]{4,3,1,2,0:T(1,128)S(1)}, u32[]{:S(2)}, u32[]{:S(2)}) %collective-permute-start.5) | collective-permute-done | bytes 81952 | tf_op jit(solution)/shard_map/ppermute | solution.py:23
  93.2 2.5 %fusion.4 = f32[640,256]{0,1:T(8,128)} fusion(f32[256,640]{1,0:T(8,128)S(1)} %fusion.80, f32[640,256]{1,0:T(8,128)} %collective-permute-done.1, s32[256]{0:T(256)S(1)} %bitcast.819, pred[256]{0:T(512)(128)(4,1)S(1)} %copy-done.102), kind=kOutput, calls=%fused_computation.23 | convolution fusion | flops 503676928 | bytes 1967360 | tf_op jit(solution)/shard_map/dot_general | solution.py:152
  95.7 2.2 %copy.371 = f32[640,256]{1,0:T(8,128)} copy(f32[640,256]{0,1:T(8,128)} %fusion.4) | data formatting | bytes 1310720 | tf_op jit(solution)/shard_map/add | solution.py:188
  97.9 2.5 %fusion.5 = f32[640,256]{0,1:T(8,128)} fusion(f32[256,640]{1,0:T(8,128)S(1)} %copy-done.24, f32[640,256]{1,0:T(8,128)} %collective-permute-done, s32[256]{0:T(256)S(1)} %bitcast.817, pred[256]{0:T(512)(128)(4,1)S(1)} %copy-done.101), kind=kOutput, calls=%fused_computation.25 | convolution fusion | flops 503676928 | bytes 1967360 | tf_op jit(solution)/shard_map/dot_general | solution.py:152
  100.5 2.2 %copy.347 = f32[640,256]{1,0:T(8,128)} copy(f32[640,256]{0,1:T(8,128)} %fusion.5) | data formatting | bytes 1310720 | tf_op jit(solution)/shard_map/add | solution.py:188
  102.6 1.9 %fusion.2 = f32[640,256]{0,1:T(8,128)S(1)} fusion(f32[256,640]{1,0:T(8,128)} %fusion.74, f32[640,256]{1,0:T(8,128)} %collective-permute-done.3, s32[256]{0:T(256)S(1)} %bitcast.815, pred[256]{0:T(512)(128)(4,1)S(1)} %copy-done.100), kind=kOutput, calls=%fused_computation.19 | convolution fusion | flops 503676928 | bytes 1967360 | tf_op jit(solution)/shard_map/dot_general | solution.py:152
  108.2 2.7 %fusion.3 = f32[640,256]{0,1:T(8,128)} fusion(f32[256,640]{1,0:T(8,128)} %fusion.77, f32[640,256]{1,0:T(8,128)} %collective-permute-done.2, s32[256]{0:T(256)S(1)} %bitcast.813, pred[256]{0:T(512)(128)(4,1)S(1)} %copy-done.99), kind=kOutput, calls=%fused_computation.21 | convolution fusion | flops 503676928 | bytes 1967360 | tf_op jit(solution)/shard_map/dot_general | solution.py:152
  111.0 2.2 %copy.391 = f32[640,256]{1,0:T(8,128)} copy(f32[640,256]{0,1:T(8,128)} %fusion.3) | data formatting | bytes 1310720 | tf_op jit(solution)/shard_map/add | solution.py:188
  113.1 2.5 %fusion.18 = (f32[5,4,4,8,256]{4,3,1,2,0:T(8,128)S(1)}, f32[5,4,4,8,256]{4,3,1,2,0:T(8,128)S(1)}, f32[5,4,4,8,256]{4,3,1,2,0:T(8,128)S(1)}) fusion(f32[5,4,4,8,256]{4,3,2,1,0:T(8,128)} %bitcast.796, f32[5,4,1,4,8,256]{5,4,3,2,1,0:T(8,128)} %get-tuple-element.161, f32[5]{0:T(128)S(1)} %compare_select_fusion.1, f32[5]{0:T(128)S(1)} %copy-done.93, ...), kind=kLoop, calls=%fused_computation.49 | loop fusion | flops 1474560 | bytes 5899836 | tf_op jit(solution)/shard_map/jit(_where)/select_n | solution.py:112
  119.4 2.0 %copy_select_fusion.2 = (f32[5,1,4,4,8,256]{5,4,2,0,1,3:T(8,128)S(1)}, f32[5,1,4,4,8,256]{5,4,2,0,1,3:T(8,128)S(1)}) fusion(f32[5,1,4,4,8,256]{5,4,3,2,0,1:T(8,128)S(1)} %bitcast.801, f32[5,1,4,4,8,256]{5,4,3,2,0,1:T(8,128)} %get-tuple-element.163, f32[5]{0:T(128)S(1)} %copy-done.93, f32[5]{0:T(128)S(1)} %compare_select_fusion.2, ...), kind=kLoop, calls=%fused_computation.81 | loop fusion | flops 2621440 | bytes 6032384 | tf_op jit(solution)/shard_map/jit(_where)/select_n | solution.py:112
  (347 shorter events, 68.0 us)
Async XLA Ops:
  0.6 11.1 %copy-start = (f32[5,4,4,4,8,256]{5,4,3,2,1,0:T(8,128)S(1)}, f32[5,4,4,4,8,256]{5,4,3,2,1,0:T(8,128)}, u32[]{:S(2)}) copy-start(f32[5,4,4,4,8,256]{5,4,3,2,1,0:T(8,128)} %param.21) | copy-start | bytes 7864324
  2.8 90.4 %collective-permute-start.1 = (f32[640,256]{1,0:T(8,128)}, f32[640,256]{1,0:T(8,128)}, u32[]{:S(2)}, u32[]{:S(2)}) collective-permute-start(f32[640,256]{1,0:T(8,128)} %bitcast.42), channel_id=1, source_target_pairs={{32,0},{40,8},{48,16},{56,24},{64,32},{72,40},{80,48},{88,56},{96,... | collective-permute-start | bytes 1966088 | tf_op jit(solution)/shard_map/ppermute | solution.py:31
  7.0 90.9 %collective-permute-start = (f32[640,256]{1,0:T(8,128)}, f32[640,256]{1,0:T(8,128)}, u32[]{:S(2)}, u32[]{:S(2)}) collective-permute-start(f32[640,256]{1,0:T(8,128)} %bitcast.15), channel_id=1, source_target_pairs={{0,32},{8,40},{16,48},{24,56},{32,64},{40,72},{48,80},{56,88},{64,... | collective-permute-start | bytes 1966088 | tf_op jit(solution)/shard_map/ppermute | solution.py:31
  13.0 89.6 %collective-permute-start.3 = (f32[640,256]{1,0:T(8,128)}, f32[640,256]{1,0:T(8,128)}, u32[]{:S(2)}, u32[]{:S(2)}) collective-permute-start(f32[640,256]{1,0:T(8,128)} %bitcast.94), channel_id=1, source_target_pairs={{8,0},{16,8},{24,16},{32,24},{40,32},{48,40},{56,48},{64,56},{72,6... | collective-permute-start | bytes 1966088 | tf_op jit(solution)/shard_map/ppermute | solution.py:31
  15.9 92.3 %collective-permute-start.2 = (f32[640,256]{1,0:T(8,128)}, f32[640,256]{1,0:T(8,128)}, u32[]{:S(2)}, u32[]{:S(2)}) collective-permute-start(f32[640,256]{1,0:T(8,128)} %bitcast.68), channel_id=1, source_target_pairs={{0,8},{8,16},{16,24},{24,32},{32,40},{40,48},{48,56},{56,64},{64,7... | collective-permute-start | bytes 1966088 | tf_op jit(solution)/shard_map/ppermute | solution.py:31
  20.8 57.8 %collective-permute-start.4 = (f32[5,4,4,1,256]{4,3,1,2,0:T(1,128)S(1)}, f32[5,4,4,1,256]{4,3,1,2,0:T(1,128)}, u32[]{:S(2)}, u32[]{:S(2)}) collective-permute-start(f32[5,4,4,1,256]{4,3,1,2,0:T(1,128)S(1)} %slice.999), channel_id=1, source_target_pairs={{0,1},{1,2},{2,3},{3,4},{4,5},{5,6},{6,7},{8,9},{9,10},{10,11},{11... | collective-permute-start | bytes 245768 | tf_op jit(solution)/shard_map/ppermute | solution.py:22
  58.1 6.4 %copy-start.83 = (f32[1,4,4,1,8,256]{5,4,3,2,1,0:T(8,128)S(1)}, f32[1,4,4,1,8,256]{5,4,3,2,1,0:T(8,128)}, u32[]{:S(2)}) copy-start(f32[1,4,4,1,8,256]{5,4,3,2,1,0:T(8,128)} %get-tuple-element.136) | copy-start | bytes 393220
  58.2 6.4 %copy-start.14 = (f32[1,4,4,1,8,256]{5,4,3,2,1,0:T(8,128)S(1)}, f32[1,4,4,1,8,256]{5,4,3,2,1,0:T(8,128)}, u32[]{:S(2)}) copy-start(f32[1,4,4,1,8,256]{5,4,3,2,1,0:T(8,128)} %get-tuple-element.139) | copy-start | bytes 393220
  58.2 6.4 %copy-start.43 = (f32[1,4,4,1,8,256]{5,4,3,2,1,0:T(8,128)S(1)}, f32[1,4,4,1,8,256]{5,4,3,2,1,0:T(8,128)}, u32[]{:S(2)}) copy-start(f32[1,4,4,1,8,256]{5,4,3,2,1,0:T(8,128)} %get-tuple-element.137) | copy-start | bytes 393220
  58.2 6.4 %copy-start.53 = (f32[1,4,4,1,8,256]{5,4,3,2,1,0:T(8,128)S(1)}, f32[1,4,4,1,8,256]{5,4,3,2,1,0:T(8,128)}, u32[]{:S(2)}) copy-start(f32[1,4,4,1,8,256]{5,4,3,2,1,0:T(8,128)} %get-tuple-element.141) | copy-start | bytes 393220
  70.7 6.8 %copy-start.20 = (f32[3,4,4,8,256]{4,3,1,2,0:T(8,128)}, f32[3,4,4,8,256]{4,3,1,2,0:T(8,128)S(1)}, u32[]{:S(2)}) copy-start(f32[3,4,4,8,256]{4,3,1,2,0:T(8,128)S(1)} %get-tuple-element.125) | copy-start | bytes 1179652
  70.7 6.8 %copy-start.38 = (f32[4,4,8,256]{3,2,0,1:T(8,128)}, f32[4,4,8,256]{3,2,0,1:T(8,128)S(1)}, u32[]{:S(2)}) copy-start(f32[4,4,8,256]{3,2,0,1:T(8,128)S(1)} %get-tuple-element.124) | copy-start | bytes 393220
  70.8 6.8 %copy-start.45 = (f32[3,4,1,4,8,256]{5,4,3,2,1,0:T(8,128)S(1)}, f32[3,4,1,4,8,256]{5,4,3,2,1,0:T(8,128)}, u32[]{:S(2)}) copy-start(f32[3,4,1,4,8,256]{5,4,3,2,1,0:T(8,128)} %get-tuple-element.159) | copy-start | bytes 1179652
  70.8 6.8 %copy-start.85 = (f32[1,4,1,4,8,256]{5,4,1,3,2,0:T(8,128)S(1)}, f32[1,4,1,4,8,256]{5,4,1,3,2,0:T(8,128)}, u32[]{:S(2)}) copy-start(f32[1,4,1,4,8,256]{5,4,1,3,2,0:T(8,128)} %copy.941) | copy-start | bytes 393220
  71.2 6.4 %copy-start.78 = (f32[1,4,1,4,8,256]{5,4,3,2,1,0:T(8,128)S(1)}, f32[1,4,1,4,8,256]{5,4,3,2,1,0:T(8,128)}, u32[]{:S(2)}) copy-start(f32[1,4,1,4,8,256]{5,4,3,2,1,0:T(8,128)} %get-tuple-element.156) | copy-start | bytes 393220
  71.3 6.4 %copy-start.7 = (f32[1,4,1,4,8,256]{5,4,3,2,1,0:T(8,128)S(1)}, f32[1,4,1,4,8,256]{5,4,3,2,1,0:T(8,128)}, u32[]{:S(2)}) copy-start(f32[1,4,1,4,8,256]{5,4,3,2,1,0:T(8,128)} %get-tuple-element.155) | copy-start | bytes 393220
  71.3 6.4 %copy-start.28 = (f32[1,4,1,4,8,256]{5,4,3,2,1,0:T(8,128)S(1)}, f32[1,4,1,4,8,256]{5,4,3,2,1,0:T(8,128)}, u32[]{:S(2)}) copy-start(f32[1,4,1,4,8,256]{5,4,3,2,1,0:T(8,128)} %get-tuple-element.154) | copy-start | bytes 393220
  71.3 6.4 %copy-start.50 = (f32[1,4,1,4,8,256]{5,4,3,2,1,0:T(8,128)S(1)}, f32[1,4,1,4,8,256]{5,4,3,2,1,0:T(8,128)}, u32[]{:S(2)}) copy-start(f32[1,4,1,4,8,256]{5,4,3,2,1,0:T(8,128)} %get-tuple-element.157) | copy-start | bytes 393220
  80.5 9.7 %copy-start.93 = (f32[5]{0:T(128)S(1)}, f32[5]{0:T(128)}, u32[]{:S(2)}) copy-start(f32[5]{0:T(128)} %constant.270.clone) | copy-start | bytes 64
  81.4 8.8 %collective-permute-start.5 = (f32[5,4,4,1,256]{4,3,1,2,0:T(1,128)S(1)}, f32[5,4,4,1,256]{4,3,1,2,0:T(1,128)S(1)}, u32[]{:S(2)}, u32[]{:S(2)}) collective-permute-start(f32[5,4,4,1,256]{4,3,1,2,0:T(1,128)S(1)} %get-tuple-element.210), channel_id=1, source_target_pairs={{1,0},{2,1},{3,2},{4,3},{5,4},{6,5},{7,6},{9,8},{10,9},{11,10},{12... | collective-permute-start | bytes 245768 | tf_op jit(solution)/shard_map/ppermute | solution.py:23
  83.7 7.8 %copy-start.71 = (f32[5,4,4,1,8,256]{5,4,1,2,3,0:T(8,128)}, f32[5,4,4,1,8,256]{5,4,1,2,3,0:T(8,128)S(1)}, u32[]{:S(2)}) copy-start(f32[5,4,4,1,8,256]{5,4,1,2,3,0:T(8,128)S(1)} %constant_dynamic-update-slice_fusion.45) | copy-start | bytes 1966084
  91.5 6.4 %copy-start.24 = (f32[256,640]{1,0:T(8,128)S(1)}, f32[256,640]{1,0:T(8,128)}, u32[]{:S(2)}) copy-start(f32[256,640]{1,0:T(8,128)} %fusion.83) | copy-start | bytes 1966084
  91.5 6.4 %copy-start.101 = (pred[256]{0:T(512)(128)(4,1)S(1)}, pred[256]{0:T(512)(128)(4,1)}, u32[]{:S(2)}) copy-start(pred[256]{0:T(512)(128)(4,1)} %get-tuple-element.87) | copy-start | bytes 772
  95.7 6.9 %copy-start.100 = (pred[256]{0:T(512)(128)(4,1)S(1)}, pred[256]{0:T(512)(128)(4,1)}, u32[]{:S(2)}) copy-start(pred[256]{0:T(512)(128)(4,1)} %get-tuple-element.86) | copy-start | bytes 772
  (85 other events, 248.0 us)
where the time goes:
time: 137 us; the launch traced here: 136 us
  local copies, waits for them, and re-layouts  56.7 us (41%)
  other arithmetic  31.1 us (23%)
  starting transfers between devices  19.8 us (14%)
  matrix products  19.4 us (14%)
  waiting for transfers between devices  6.58 us (5%)
  between operations  2.5 us (2%)
    unnamed x226, local copies, waits for them, and re-layouts  29 us
    dot_general x8, matrix products, select_rows(): jnp.dot(source, selector, precision=lax.Precision.HIGHEST, preferred_elem...  19.4 us
    ppermute x4, starting transfers between devices, from_behind(): return lax.ppermute(array, axis, pairs)  14.3 us
    add x4, local copies, waits for them, and re-layouts, per_device(): ghost_flat = ghost_flat + select_rows(arrived, remote_select)  7.63 us
    ppermute x1, waiting for transfers between devices, extended(): after = lax.ppermute(leading, axis, down)  6.57 us
    unnamed x43, other arithmetic  6.46 us
    mul x6, other arithmetic, face_term(): common = 0.5 * (flux_in + flux_out) - 0.5 * wave_speed * (outside - inside)  6.05 us
    select_n x3, other arithmetic, outer_state(): jnp.where(face_kind == 0, ghost_side, jnp.where(face_kind == 1, mirrored(...  5.77 us
  transfers between devices with their start and end apart: 6, of which 1 were waited for; matrix products, arithmetic and copies ran while one was open for 54% of the time, Pallas kernels for 0%

commit v1 on v0

v1 whole, which is shorter than its diff:
```python
import functools

import jax
import jax.numpy as jnp
import numpy as np
from jax import lax
from jax.experimental import pallas as pl
from jax.experimental.pallas import tpu as pltpu
from jax.sharding import PartitionSpec as P

TIME_STEP = 0.02
SECTION_DECAY = -0.4178904745
SECTION_WEIGHT = 1.720146321549
LIFT = 3.0 * TIME_STEP
FREE_STREAM = (1.0, 0.3, 0.1, 0.0, 1.0 / 0.56 + 0.05)
MESH = pl.DeviceIdType.MESH
SLOTS = 16
BF16 = jnp.bfloat16
F32 = jnp.float32
STEPS = (4, -4, 1, -1)


def derivative_entries():
    nodes = np.array([-1.0, -1.0 / np.sqrt(5.0), 1.0 / np.sqrt(5.0), 1.0])
    products = np.array(
        [np.prod([nodes[t] - nodes[a] for a in range(4) if a != t]) for t in range(4)]
    )
    matrix = np.zeros((4, 4))
    for t in range(4):
        for s in range(4):
            if t != s:
                matrix[t, s] = products[t] / products[s] / (nodes[t] - nodes[s])
            else:
                matrix[t, t] = sum(1.0 / (nodes[t] - nodes[a]) for a in range(4) if a != t)
    return matrix


ENTRIES = -TIME_STEP * derivative_entries()
ODD = [[0.5 * float(ENTRIES[p, i] - ENTRIES[p, 3 - i]) for i in (0, 1)] for p in (0, 1)]
EVEN = [0.5 * float(ENTRIES[p, 0] + ENTRIES[p, 3]) for p in (0, 1)]


def derived(f):
    s0, d0 = f[0] + f[3], f[0] - f[3]
    s1, d1 = f[1] + f[2], f[1] - f[2]
    t = s0 - s1
    a = ODD[0][0] * d0 + ODD[0][1] * d1
    b = EVEN[0] * t
    c = ODD[1][0] * d0 + ODD[1][1] * d1
    e = EVEN[1] * t
    return a + b, c + e, c - e, a - b


def inverse(x):
    r = pl.reciprocal(x, approx=True)
    return r * (2.0 - x * r)


def split(x):
    hi = x.astype(BF16)
    lo = (x - hi.astype(F32)).astype(BF16)
    return hi, lo


def dot(a, b):
    return jnp.dot(a, b, preferred_element_type=F32)


def dot_nt(a, b):
    return lax.dot_general(a, b, (((1,), (1,)), ((), ())), preferred_element_type=F32)


def trace_of(cv, side):
    face = (0, 3)[side % 2]
    block = cv[:, face] if side < 2 else cv[:, :, face]
    return block.reshape(640, 256)


def exchange_kernel(
    cons, reg, nb, cv, acc, ghost, vert,
    prim, stage, packed, arrived, sendv, recvv, load_sem, send_sem, recv_sem, vsend_sem, vrecv_sem,
):
    foot, layer = lax.axis_index("foot"), lax.axis_index("layer")
    feet, layers = lax.axis_size("foot"), lax.axis_size("layer")

    def at_foot(by):
        return (lax.rem(foot + by + feet, feet), layer)

    def at_layer(by):
        return (foot, lax.rem(layer + by + layers, layers))

    loads = [pltpu.make_async_copy(cons.at[v], cv.at[v], load_sem.at[v]) for v in range(5)]
    for copy in loads:
        copy.start()
    reg_load = pltpu.make_async_copy(reg, acc, load_sem.at[5])
    reg_load.start()

    barrier = pltpu.get_barrier_semaphore()
    partners = [at_foot(by) for by in STEPS] + [at_layer(by) for by in (1, -1)]
    for partner in partners:
        pl.semaphore_signal(barrier, inc=1, device_id=partner, device_id_type=MESH)

    here = nb[...] - foot * 256
    remote = jnp.logical_or(here < 0, here >= 256)
    mask = jnp.where(remote, 1.0, 0.0)
    mask8 = jnp.concatenate([mask, jnp.zeros_like(mask)], axis=0).astype(BF16)
    rows = lax.broadcasted_iota(jnp.int32, (256, 256), 0)
    cols = lax.broadcasted_iota(jnp.int32, (256, 256), 1)
    before = jnp.where(rows < cols, 1.0, 0.0).astype(BF16)
    rank = dot(mask8, before)
    rank = jnp.where(mask8.astype(F32) > 0.5, rank, -1.0).astype(jnp.int32)
    named = (lax.bitwise_and(nb[...], 255) + 1).astype(F32)
    named8 = jnp.concatenate([named, jnp.zeros_like(named)], axis=0).astype(BF16)
    slot = lax.bitwise_and(lax.broadcasted_iota(jnp.int32, (128, 256), 0), SLOTS - 1)
    lane_z = lax.broadcasted_iota(jnp.int32, (80, 128), 1) // SLOTS

    for copy in loads:
        copy.wait()
    pl.semaphore_wait(barrier, len(partners))

    vcopies = []
    for way in (0, 1):
        for h in (0, 1):
            lanes = pl.ds(h * 128, 128)
            stage[2 * way + h] = cv[:, :, :, pl.ds(24 * way, 8), lanes].reshape(640, 128)
            sendv[way, :, lanes] = stage[2 * way + h, pl.ds(7 * way, 80, stride=8), :]
        copy = pltpu.make_async_remote_copy(
            src_ref=sendv.at[way], dst_ref=recvv.at[way], send_sem=vsend_sem.at[way],
            recv_sem=vrecv_sem.at[way], device_id=at_layer((-1, 1)[way]), device_id_type=MESH,
        )
        copy.start()
        vcopies.append(copy)

    copies = []
    for side in range(4):
        q = side ^ 1
        hi, lo = split(trace_of(cv, q))
        pick = jnp.where(rank[q:q + 1] == slot, 1.0, 0.0).astype(BF16)
        stage[side] = dot_nt(hi, pick) + dot_nt(lo, pick)
        total = stage[side, pl.ds(0, 80, stride=8), :]
        for z in range(1, 8):
            total = jnp.where(lane_z == z, stage[side, pl.ds(z, 80, stride=8), :], total)
        packed[side, 0:80] = total
        packed[side, 80:88] = dot_nt(named8, pick)
        copy = pltpu.make_async_remote_copy(
            src_ref=packed.at[side], dst_ref=arrived.at[side], send_sem=send_sem.at[side],
            recv_sem=recv_sem.at[side], device_id=at_foot(STEPS[side]), device_id_type=MESH,
        )
        copy.start()
        copies.append(copy)
        select = jnp.where(here[side:side + 1] == rows, 1.0, 0.0).astype(BF16)
        ghost[side] = (dot(hi, select) + dot(lo, select)).reshape(5, 4, 32, 256)

    reg_load.wait()

    def z_lines(line, carry):
        i, j = line // 4, line % 4
        q = [[cv[v, i, j, pl.ds(8 * k, 8), :] for k in range(4)] for v in range(5)]
        flux = [[], [], [], [], []]
        for k in range(4):
            rho, mx, my, mz, energy = (q[v][k] for v in range(5))
            r = inverse(rho)
            kinetic = (mx * mx + my * my + mz * mz) * r
            pressure = 0.4 * energy - 0.2 * kinetic
            vz = mz * r
            rows_k = pl.ds(8 * k, 8)
            prim[0, i, j, rows_k, :] = mx * r
            prim[1, i, j, rows_k, :] = my * r
            prim[2, i, j, rows_k, :] = pressure
            flux[0].append(mz)
            flux[1].append(mx * vz)
            flux[2].append(my * vz)
            flux[3].append(mz * vz + pressure)
            flux[4].append((energy + pressure) * vz)
        for v in range(5):
            out = derived(flux[v])
            for k in range(4):
                rows_k = pl.ds(8 * k, 8)
                acc[v, i, j, rows_k, :] = SECTION_DECAY * acc[v, i, j, rows_k, :] + out[k]
        return carry

    lax.fori_loop(0, 16, z_lines, 0)

    def lines(direction, line, carry):
        a, k = line // 4, line % 4
        rows_k = pl.ds(pl.multiple_of(8 * k, 8), 8)

        def at(node):
            return (node, a, rows_k, slice(None)) if direction == 0 else (a, node, rows_k, slice(None))

        flux = [[], [], [], [], []]
        for node in range(4):
            vd = prim[(direction,) + at(node)]
            pressure = prim[(2,) + at(node)]
            m = [cv[(1 + c,) + at(node)] for c in range(3)]
            flux[0].append(m[direction])
            for c in range(3):
                entry = m[c] * vd
                if c == direction:
                    entry = entry + pressure
                flux[1 + c].append(entry)
            flux[4].append((cv[(4,) + at(node)] + pressure) * vd)
        for v in range(5):
            out = derived(flux[v])
            for node in range(4):
                acc[(v,) + at(node)] = acc[(v,) + at(node)] + out[node]
        return carry

    lax.fori_loop(0, 16, functools.partial(lines, 0), 0)
    lax.fori_loop(0, 16, functools.partial(lines, 1), 0)

    lane_z3 = lax.broadcasted_iota(jnp.int32, (80, 8, 128), 2) // SLOTS
    sub_z3 = lax.broadcasted_iota(jnp.int32, (80, 8, 128), 1)
    column = (lax.broadcasted_iota(jnp.int32, (256, 128), 0) + 1).astype(F32)
    for side in range(4):
        copies[side].wait()
        q = side ^ 1
        place = jnp.where(arrived[side, 80 + q:81 + q] == column, 1.0, 0.0).astype(BF16)
        spread = jnp.where(lane_z3 == sub_z3, arrived[side, 0:80][:, None, :], 0.0).reshape(640, 128)
        hi, lo = split(spread)
        both = jnp.concatenate([hi, lo], axis=1)
        twice = jnp.concatenate([place, place], axis=1)
        ghost[side] = ghost[side] + dot_nt(both, twice).reshape(5, 4, 32, 256)

    for copy in vcopies:
        copy.wait()
    lowest, highest = layer == 0, layer == layers - 1
    for v in range(5):
        part = pl.ds(16 * v, 16)
        own = sendv[0, part, :]
        vert[0, part, :] = jnp.where(lowest, -own if v == 3 else own, recvv[1, part, :])
        vert[1, part, :] = jnp.where(highest, jnp.full_like(own, FREE_STREAM[v]), recvv[0, part, :])


def state(q, direction, need_all=False):
    rho, energy = q[0], q[4]
    r = inverse(rho)
    kinetic = (q[1] * q[1] + q[2] * q[2] + q[3] * q[3]) * r
    pressure = 0.4 * energy - 0.2 * kinetic
    square = 1.4 * pressure * r
    sound = square * lax.rsqrt(square)
    return r, pressure, sound


def surface_kernel(cv, acc, ghost, vert, kinds, adv, new, adv_v, new_v, out_sem):
    sub = lax.broadcasted_iota(jnp.int32, (8, 128), 0)
    outs = []
    for i in range(4):

        def half(h, carry):
            lanes = pl.ds(pl.multiple_of(h * 128, 128), 128)
            kind = [jnp.broadcast_to(kinds[s:s + 1, lanes], (8, 128)) for s in range(4)]
            open_face = [kind[s] == 0 for s in range(4)]
            wall = [kind[s] == 1 for s in range(4)]
            for j in range(4):
                for k in range(4):
                    rows_k = pl.ds(8 * k, 8)
                    q = [cv[v, i, j, rows_k, lanes] for v in range(5)]
                    total = [acc[v, i, j, rows_k, lanes] for v in range(5)]
                    faces = []
                    if i in (0, 3):
                        faces.append((0, 0 if i == 0 else 1, (j, k)))
                    if j in (0, 3):
                        faces.append((1, 2 if j == 0 else 3, (i, k)))
                    if k in (0, 3):
                        faces.append((2, 4 if k == 0 else 5, (i, j)))
                    if faces:
                        r_in, p_in, c_in = state(q, 0)
                    for d, side, (a, b) in faces:
                        if side < 4:
                            outer = []
                            for v in range(5):
                                inner = -q[v] if v == 1 + d else q[v]
                                other = jnp.where(wall[side], inner, FREE_STREAM[v])
                                got = ghost[side, v, a, pl.ds(8 * b, 8), lanes]
                                outer.append(jnp.where(open_face[side], got, other))
                        else:
                            outer = []
                            for v in range(5):
                                m = v * 16 + a * 4 + b
                                if side == 4:
                                    near = cv[v, i, j, pl.ds(24, 8), lanes]
                                    near = pltpu.roll(near, 1, 0)
                                    edge = jnp.broadcast_to(vert[0, m:m + 1, lanes], (8, 128))
                                    outer.append(jnp.where(sub == 0, edge, near))
                                else:
                                    near = cv[v, i, j, pl.ds(0, 8), lanes]
                                    near = pltpu.roll(near, 7, 0)
                                    edge = jnp.broadcast_to(vert[1, m:m + 1, lanes], (8, 128))
                                    outer.append(jnp.where(sub == 7, edge, near))
                        sign = -1.0 if side % 2 == 0 else 1.0
                        r_out, p_out, c_out = state(outer, d)
                        v_in, v_out = q[1 + d] * r_in, outer[1 + d] * r_out
                        lam = LIFT * jnp.maximum(jnp.abs(v_in) + c_in, jnp.abs(v_out) + c_out)
                        s_in, s_out = (sign * LIFT) * v_in, (sign * LIFT) * v_out
                        w_in, w_out = lam - s_in, lam - s_out
                        for v in range(5):
                            total[v] = total[v] + (w_out * outer[v] - w_in * q[v])
                        total[1 + d] = total[1 + d] - (sign * LIFT) * (p_out - p_in)
                        total[4] = total[4] - (p_out * s_out - p_in * s_in)
                    for v in range(5):
                        new_v[v, i, j, rows_k, lanes] = total[v]
                        adv_v[v, i, j, rows_k, lanes] = q[v] + SECTION_WEIGHT * total[v]
            return carry

        lax.fori_loop(0, 2, half, 0)
        for n, (src, dst) in enumerate(((adv_v, adv), (new_v, new))):
            copy = pltpu.make_async_copy(src.at[:, i], dst.at[:, i], out_sem.at[n, i])
            copy.start()
            outs.append(copy)
    for copy in outs:
        copy.wait()


def per_device(conserved, register, neighbour, side_type):
    shape = (5, 4, 4, 32, 256)
    cons, reg = conserved.reshape(shape), register.reshape(shape)
    cv, acc, ghost, vert = pl.pallas_call(
        exchange_kernel,
        name="exchange",
        out_shape=(
            pltpu.VMEM(shape, F32),
            pltpu.VMEM(shape, F32),
            pltpu.VMEM((4, 5, 4, 32, 256), F32),
            pltpu.VMEM((2, 80, 256), F32),
        ),
        in_specs=[
            pl.BlockSpec(memory_space=pl.ANY),
            pl.BlockSpec(memory_space=pl.ANY),
            pl.BlockSpec(memory_space=pltpu.VMEM),
        ],
        out_specs=tuple([pl.BlockSpec(memory_space=pltpu.VMEM)] * 4),
        scratch_shapes=[
            pltpu.VMEM((3, 4, 4, 32, 256), F32),
            pltpu.VMEM((4, 640, 128), F32),
            pltpu.VMEM((4, 88, 128), F32),
            pltpu.VMEM((4, 88, 128), F32),
            pltpu.VMEM((2, 80, 256), F32),
            pltpu.VMEM((2, 80, 256), F32),
            pltpu.SemaphoreType.DMA((6,)),
            pltpu.SemaphoreType.DMA((4,)),
            pltpu.SemaphoreType.DMA((4,)),
            pltpu.SemaphoreType.DMA((2,)),
            pltpu.SemaphoreType.DMA((2,)),
        ],
        compiler_params=pltpu.CompilerParams(
            collective_id=0, has_side_effects=True, vmem_limit_bytes=40 * 1024 * 1024
        ),
    )(cons, reg, neighbour)
    cv, acc, ghost, vert = (
        pltpu.with_memory_space_constraint(x, pltpu.VMEM) for x in (cv, acc, ghost, vert)
    )
    adv, new = pl.pallas_call(
        surface_kernel,
        name="surface",
        out_shape=(jax.ShapeDtypeStruct(shape, F32), jax.ShapeDtypeStruct(shape, F32)),
        in_specs=[pl.BlockSpec(memory_space=pltpu.VMEM)] * 5,
        out_specs=(pl.BlockSpec(memory_space=pl.ANY), pl.BlockSpec(memory_space=pl.ANY)),
        scratch_shapes=[
            pltpu.VMEM(shape, F32),
            pltpu.VMEM(shape, F32),
            pltpu.SemaphoreType.DMA((2, 4)),
        ],
        compiler_params=pltpu.CompilerParams(vmem_limit_bytes=32 * 1024 * 1024),
    )(cv, acc, ghost, vert, side_type)
    full = (5, 4, 4, 4, 8, 256)
    return adv.reshape(full), new.reshape(full)


def solution(mesh):
    spec = P(None, None, None, None, "layer", "foot")
    return jax.shard_map(
        per_device,
        mesh=mesh,
        in_specs=(spec, spec, P(None, "foot"), P(None, "foot")),
        out_specs=(spec, spec),
        check_vma=False,
    )
```

time: 137 us -> 24.4 us (0.18)
  the two profiles are of different devices: /device:TPU:123 before, /device:TPU:1 now
where the time goes in v1:
time: 24.4 us; the launch traced here: 24.2 us
  Pallas kernels  19.4 us (80%)
  local copies, waits for them, and re-layouts  4.16 us (17%)
  between operations  0.66 us (3%)
    pallas_call x1, Pallas kernels, per_device(): pl.pallas_call(exchange_kernel, name='exchange', out_shape=(pltpu.VMEM(sh...  15.8 us
    unnamed x8, local copies, waits for them, and re-layouts  4.16 us
    pallas_call x1, Pallas kernels, per_device(): pl.pallas_call(surface_kernel, name='surface', out_shape=(jax.ShapeDtypeS...  3.55 us

profile of v1, /device:TPU:1, one launch (start us, length us, event | category | flops | bytes accessed | tf_op | source)
XLA Modules:
  0.0 24.2 jit_solution(11486753934489237514)
XLA Ops:
  0.6 0.0 copy-start
  0.6 1.7 %copy-done = f32[5,4,4,4,8,256]{5,4,3,2,1,0:T(8,128)S(1)} copy-done((f32[5,4,4,4,8,256]{5,4,3,2,1,0:T(8,128)S(1)}, f32[5,4,4,4,8,256]{5,4,3,2,1,0:T(8,128)}, u32[]{:S(2)}) %copy-start) | copy-done | bytes 2621464
  2.4 0.0 copy-start.1
  2.4 1.7 %copy-done.1 = f32[5,4,4,4,8,256]{5,4,3,2,1,0:T(8,128)S(1)} copy-done((f32[5,4,4,4,8,256]{5,4,3,2,1,0:T(8,128)S(1)}, f32[5,4,4,4,8,256]{5,4,3,2,1,0:T(8,128)}, u32[]{:S(2)}) %copy-start.1) | copy-done | bytes 2621464
  4.1 0.0 copy-start.3
  4.1 0.7 %copy-done.3 = s32[4,256]{1,0:T(4,128)S(1)} copy-done((s32[4,256]{1,0:T(4,128)S(1)}, s32[4,256]{1,0:T(4,128)}, u32[]{:S(2)}) %copy-start.3) | copy-done | bytes 4120
  4.8 0.0 copy-start.2
  4.8 15.8 %exchange.1 = (f32[5,4,4,32,256]{4,3,2,1,0:T(8,128)S(1)}, f32[5,4,4,32,256]{4,3,2,1,0:T(8,128)S(1)}, f32[4,5,4,32,256]{4,3,2,1,0:T(8,128)S(1)}, f32[2,80,256]{2,1,0:T(8,128)S(1)}) custom-call(f32[5,4,4,32,256]{4,3,2,1,0:T(8,128)S(1)} %bitcast.4, f32[5,4,4,32,256]{4,3,2,1,0:T(8,128)S(1)} %bitcast.5, s32[4,256]{1,0:T(4,128)S(1)} %copy-done.3), custom_call_target="tpu_custom_call" | custom-call | tf_op jit(solution)/shard_map/exchange/pallas_call | solution.py:318
  20.6 0.0 copy-done.2
  20.6 3.5 %surface.1 = (f32[5,4,4,32,256]{4,3,2,1,0:T(8,128)}, f32[5,4,4,32,256]{4,3,2,1,0:T(8,128)}) custom-call(f32[5,4,4,32,256]{4,3,2,1,0:T(8,128)S(1)} %get-tuple-element.8.cv, f32[5,4,4,32,256]{4,3,2,1,0:T(8,128)S(1)} %get-tuple-element.9.acc, f32[4,5,4,32,256]{4,3,2,1,0:T(8,128)S(1)} %get-tuple-element.10.ghost, f32[2,80,256]{2,1,0:T(8,128)S(1)} %get-tuple-element.11.vert, ...), custom_call_target="tpu_custom_call" | custom-call | tf_op jit(solution)/shard_map/surface/pallas_call | solution.py:353
Async XLA Ops:
  0.6 1.7 %copy-start = (f32[5,4,4,4,8,256]{5,4,3,2,1,0:T(8,128)S(1)}, f32[5,4,4,4,8,256]{5,4,3,2,1,0:T(8,128)}, u32[]{:S(2)}) copy-start(f32[5,4,4,4,8,256]{5,4,3,2,1,0:T(8,128)} %param.4) | copy-start | bytes 7864324
  2.4 1.7 %copy-start.1 = (f32[5,4,4,4,8,256]{5,4,3,2,1,0:T(8,128)S(1)}, f32[5,4,4,4,8,256]{5,4,3,2,1,0:T(8,128)}, u32[]{:S(2)}) copy-start(f32[5,4,4,4,8,256]{5,4,3,2,1,0:T(8,128)} %param.5) | copy-start | bytes 7864324
  4.1 0.7 %copy-start.3 = (s32[4,256]{1,0:T(4,128)S(1)}, s32[4,256]{1,0:T(4,128)}, u32[]{:S(2)}) copy-start(s32[4,256]{1,0:T(4,128)} %nb.1) | copy-start | bytes 12292
  4.8 15.8 %copy-start.2 = (s32[4,256]{1,0:T(4,128)S(1)}, s32[4,256]{1,0:T(4,128)}, u32[]{:S(2)}) copy-start(s32[4,256]{1,0:T(4,128)} %kinds.1) | copy-start | bytes 12292

commit v2 on v1

v2 whole, which is shorter than its diff:
```python
import functools

import jax
import jax.numpy as jnp
import numpy as np
from jax import lax
from jax.experimental import pallas as pl
from jax.experimental.pallas import tpu as pltpu
from jax.sharding import PartitionSpec as P

TIME_STEP = 0.02
SECTION_DECAY = -0.4178904745
SECTION_WEIGHT = 1.720146321549
LIFT = 3.0 * TIME_STEP
FREE_STREAM = (1.0, 0.3, 0.1, 0.0, 1.0 / 0.56 + 0.05)
MESH = pl.DeviceIdType.MESH
SLOTS = 16
BF16 = jnp.bfloat16
F32 = jnp.float32
STEPS = (4, -4, 1, -1)


def derivative_entries():
    nodes = np.array([-1.0, -1.0 / np.sqrt(5.0), 1.0 / np.sqrt(5.0), 1.0])
    products = np.array(
        [np.prod([nodes[t] - nodes[a] for a in range(4) if a != t]) for t in range(4)]
    )
    matrix = np.zeros((4, 4))
    for t in range(4):
        for s in range(4):
            if t != s:
                matrix[t, s] = products[t] / products[s] / (nodes[t] - nodes[s])
            else:
                matrix[t, t] = sum(1.0 / (nodes[t] - nodes[a]) for a in range(4) if a != t)
    return matrix


ENTRIES = -TIME_STEP * derivative_entries()
ODD = [[0.5 * float(ENTRIES[p, i] - ENTRIES[p, 3 - i]) for i in (0, 1)] for p in (0, 1)]
EVEN = [0.5 * float(ENTRIES[p, 0] + ENTRIES[p, 3]) for p in (0, 1)]


def derived(f):
    s0, d0 = f[0] + f[3], f[0] - f[3]
    s1, d1 = f[1] + f[2], f[1] - f[2]
    t = s0 - s1
    a = ODD[0][0] * d0 + ODD[0][1] * d1
    b = EVEN[0] * t
    c = ODD[1][0] * d0 + ODD[1][1] * d1
    e = EVEN[1] * t
    return a + b, c + e, c - e, a - b


def inverse(x):
    r = pl.reciprocal(x, approx=True)
    return r * (2.0 - x * r)


def split(x):
    hi = x.astype(BF16)
    lo = (x - hi.astype(F32)).astype(BF16)
    return hi, lo


def dot(a, b):
    return jnp.dot(a, b, preferred_element_type=F32)


def dot_nt(a, b):
    return lax.dot_general(a, b, (((1,), (1,)), ((), ())), preferred_element_type=F32)


def face_rows(side):
    face = (0, 3)[side % 2]
    return (slice(None), face) if side < 2 else (slice(None), slice(None), face)


def trace_of(cv, side):
    return cv[face_rows(side)].reshape(640, 256)


def primitive(q):
    r = inverse(q[0])
    kinetic = (q[1] * q[1] + q[2] * q[2] + q[3] * q[3]) * r
    pressure = 0.4 * q[4] - 0.2 * kinetic
    square = 1.4 * pressure * r
    return r, pressure, square * lax.rsqrt(square)


def face_change(inner, outer, direction, sign, inner_known=None):
    if inner_known is None:
        r_in, p_in, c_in = primitive(inner)
        v_in = inner[1 + direction] * r_in
    else:
        v_in, p_in, c_in = inner_known
    r_out, p_out, c_out = primitive(outer)
    v_out = outer[1 + direction] * r_out
    lam = LIFT * jnp.maximum(jnp.abs(v_in) + c_in, jnp.abs(v_out) + c_out)
    s_in, s_out = (sign * LIFT) * v_in, (sign * LIFT) * v_out
    w_in, w_out = lam - s_in, lam - s_out
    change = [w_out * outer[v] - w_in * inner[v] for v in range(5)]
    change[1 + direction] = change[1 + direction] - (sign * LIFT) * (p_out - p_in)
    change[4] = change[4] - (p_out * s_out - p_in * s_in)
    return change


def gather_slots(stage, side, lane_z):
    total = stage[side, pl.ds(0, 80, stride=8), :]
    for z in range(1, 8):
        total = jnp.where(lane_z == z, stage[side, pl.ds(z, 80, stride=8), :], total)
    return total


def exchange_kernel(
    cons, reg, nb_in, kinds_in, cv, acc, lateral, vertical, picks,
    nb, kinds, prim, ghost, stage, packed, own, arrived, sendv, recvv, load_sem, send_sem, recv_sem, vsend_sem, vrecv_sem,
):
    foot, layer = lax.axis_index("foot"), lax.axis_index("layer")
    feet, layers = lax.axis_size("foot"), lax.axis_size("layer")

    def at_foot(by):
        return (lax.rem(foot + by + feet, feet), layer)

    def at_layer(by):
        return (foot, lax.rem(layer + by + layers, layers))

    barrier = pltpu.get_barrier_semaphore()
    partners = [at_foot(by) for by in STEPS] + [at_layer(by) for by in (1, -1)]
    for partner in partners:
        pl.semaphore_signal(barrier, inc=1, device_id=partner, device_id_type=MESH)
    maps = [
        pltpu.make_async_copy(nb_in, nb, load_sem.at[6]),
        pltpu.make_async_copy(kinds_in, kinds, load_sem.at[7]),
    ]
    for copy in maps:
        copy.start()
    loads = [pltpu.make_async_copy(cons.at[v], cv.at[v], load_sem.at[v]) for v in range(5)]
    for copy in loads:
        copy.start()
    reg_load = pltpu.make_async_copy(reg, acc, load_sem.at[5])
    reg_load.start()

    slot = lax.bitwise_and(lax.broadcasted_iota(jnp.int32, (128, 256), 0), SLOTS - 1)
    lane_z = lax.broadcasted_iota(jnp.int32, (80, 128), 1) // SLOTS
    rows = lax.broadcasted_iota(jnp.int32, (256, 256), 0)
    cols = lax.broadcasted_iota(jnp.int32, (256, 256), 1)
    before = jnp.where(rows < cols, 1.0, 0.0).astype(BF16)
    for copy in maps:
        copy.wait()
    here = nb[...] - foot * 256
    mask = jnp.where(jnp.logical_or(here < 0, here >= 256), 1.0, 0.0)
    mask8 = jnp.concatenate([mask, jnp.zeros_like(mask)], axis=0).astype(BF16)
    rank = jnp.where(mask8.astype(F32) > 0.5, dot(mask8, before), -1.0).astype(jnp.int32)

    for copy in loads:
        copy.wait()

    for way in (0, 1):
        for h in (0, 1):
            lanes = pl.ds(h * 128, 128)
            stage[2 * way + h] = cv[:, :, :, pl.ds(24 * way, 8), lanes].reshape(640, 128)
            sendv[way, :, lanes] = stage[2 * way + h, pl.ds(7 * way, 80, stride=8), :]
    for side in range(4):
        hi, lo = split(trace_of(cv, side ^ 1))
        pick = jnp.where(rank[(side ^ 1):(side ^ 1) + 1] == slot, 1.0, 0.0).astype(BF16)
        stage[side] = dot_nt(hi, pick) + dot_nt(lo, pick)
        packed[side] = gather_slots(stage, side, lane_z)

    pl.semaphore_wait(barrier, len(partners))
    copies = []
    for side in range(4):
        copies.append(pltpu.make_async_remote_copy(
            src_ref=packed.at[side], dst_ref=arrived.at[side], send_sem=send_sem.at[side],
            recv_sem=recv_sem.at[side], device_id=at_foot(STEPS[side]), device_id_type=MESH,
        ))
    for way in (0, 1):
        copies.append(pltpu.make_async_remote_copy(
            src_ref=sendv.at[way], dst_ref=recvv.at[way], send_sem=vsend_sem.at[way],
            recv_sem=vrecv_sem.at[way], device_id=at_layer((-1, 1)[way]), device_id_type=MESH,
        ))
    for copy in copies:
        copy.start()

    reg_load.wait()

    def z_lines(line, carry):
        i, j = line // 4, line % 4
        q = [[cv[v, i, j, pl.ds(8 * k, 8), :] for k in range(4)] for v in range(5)]
        flux = [[], [], [], [], []]
        for k in range(4):
            rho, mx, my, mz, energy = (q[v][k] for v in range(5))
            r, pressure, sound = primitive([q[v][k] for v in range(5)])
            vz = mz * r
            rows_k = pl.ds(8 * k, 8)
            prim[0, i, j, rows_k, :] = mx * r
            prim[1, i, j, rows_k, :] = my * r
            prim[2, i, j, rows_k, :] = vz
            prim[3, i, j, rows_k, :] = pressure
            prim[4, i, j, rows_k, :] = sound
            flux[0].append(mz)
            flux[1].append(mx * vz)
            flux[2].append(my * vz)
            flux[3].append(mz * vz + pressure)
            flux[4].append((energy + pressure) * vz)
        for v in range(5):
            out = derived(flux[v])
            for k in range(4):
                rows_k = pl.ds(8 * k, 8)
                acc[v, i, j, rows_k, :] = SECTION_DECAY * acc[v, i, j, rows_k, :] + out[k]
        return carry

    lax.fori_loop(0, 16, z_lines, 0)

    def lines(direction, line, carry):
        a, k = line // 4, line % 4
        rows_k = pl.ds(pl.multiple_of(8 * k, 8), 8)

        def at(node):
            return (node, a, rows_k, slice(None)) if direction == 0 else (a, node, rows_k, slice(None))

        flux = [[], [], [], [], []]
        for node in range(4):
            vd = prim[(direction,) + at(node)]
            pressure = prim[(3,) + at(node)]
            m = [cv[(1 + c,) + at(node)] for c in range(3)]
            flux[0].append(m[direction])
            for c in range(3):
                entry = m[c] * vd
                if c == direction:
                    entry = entry + pressure
                flux[1 + c].append(entry)
            flux[4].append((cv[(4,) + at(node)] + pressure) * vd)
        for v in range(5):
            out = derived(flux[v])
            for node in range(4):
                acc[(v,) + at(node)] = acc[(v,) + at(node)] + out[node]
        return carry

    lax.fori_loop(0, 16, functools.partial(lines, 0), 0)
    lax.fori_loop(0, 16, functools.partial(lines, 1), 0)

    kind = kinds[...]
    open_face = kind == 0
    for side in range(4):
        hi, lo = split(trace_of(cv, side ^ 1))
        select = jnp.where(here[side:side + 1] == rows, 1.0, 0.0).astype(BF16)
        ghost[...] = (dot(hi, select) + dot(lo, select)).reshape(5, 4, 32, 256)
        local = jnp.broadcast_to(jnp.where(open_face, 1.0 - mask, 0.0)[side:side + 1], (8, 256)) > 0.5
        far = jnp.broadcast_to(kind[side:side + 1], (8, 256)) == 2
        flip = jnp.broadcast_to(jnp.where(kind == 1, -1.0, 1.0)[side:side + 1], (8, 256))
        d, face, sign = side // 2, (0, 3)[side % 2], (-1.0, 1.0)[side % 2]

        def lateral_nodes(node, carry):
            a, b = node // 4, node % 4
            rows_b = pl.ds(pl.multiple_of(8 * b, 8), 8)
            at = (face, a, rows_b, slice(None)) if d == 0 else (a, face, rows_b, slice(None))
            q = [cv[(v,) + at] for v in range(5)]
            outer = []
            for v in range(5):
                inner = q[v] * flip if v == 1 + d else q[v]
                outer.append(jnp.where(local, ghost[v, a, rows_b, :], jnp.where(far, FREE_STREAM[v], inner)))
            known = prim[(d,) + at], prim[(3,) + at], prim[(4,) + at]
            change = face_change(q, outer, d, sign, known)
            for v in range(5):
                acc[(v,) + at] = acc[(v,) + at] + change[v]
            return carry

        lax.fori_loop(0, 16, lateral_nodes, 0, unroll=2)

        named = lax.bitwise_and(nb[side:side + 1], 255)
        named = jnp.where(mask[side:side + 1] > 0.5, named, -1)
        onehot = jnp.where(rows == named, 1.0, 0.0).astype(BF16)
        hit = dot_nt(jnp.ones((8, 256), BF16), onehot).astype(BF16)
        order = dot(dot(hit, before).astype(BF16), onehot)
        order = jnp.where(jnp.logical_and(open_face, mask > 0.5)[side:side + 1], order[0:1], -1.0)
        pick = jnp.where(order.astype(jnp.int32) == slot, 1.0, 0.0).astype(BF16)
        picks[side] = pick
        hi, lo = split(trace_of(cv, side))
        stage[side] = dot_nt(hi, pick) + dot_nt(lo, pick)
        own[side, 0:80] = gather_slots(stage, side, lane_z)
        own[side, 80:88] = dot_nt(jnp.ones((8, 256), BF16), pick)

    sub = lax.broadcasted_iota(jnp.int32, (8, 256), 0)
    for way in (0, 1):
        rows_here, rows_there = (pl.ds(0, 8), pl.ds(24, 8)) if way == 0 else (pl.ds(24, 8), pl.ds(0, 8))
        shift, edge, sign = (1, 0, -1.0) if way == 0 else (7, 7, 1.0)

        def vertical_nodes(node, carry):
            at = (node // 4, node % 4, rows_here, slice(None))
            there = (node // 4, node % 4, rows_there, slice(None))
            q = [cv[(v,) + at] for v in range(5)]
            outer = [jnp.where(sub == edge, q[v], pltpu.roll(cv[(v,) + there], shift, 0)) for v in range(5)]
            known = prim[(2,) + at], prim[(3,) + at], prim[(4,) + at]
            change = face_change(q, outer, 2, sign, known)
            for v in range(5):
                acc[(v,) + at] = acc[(v,) + at] + change[v]
            return carry

        lax.fori_loop(0, 16, vertical_nodes, 0, unroll=2)

    for copy in copies:
        copy.wait()

    for side in range(4):
        valid = jnp.broadcast_to(own[side, 80:81] > 0.5, (16, 128))
        inner = [jnp.where(valid, own[side, 16 * v:16 * v + 16], FREE_STREAM[v]) for v in range(5)]
        outer = [jnp.where(valid, arrived[side, 16 * v:16 * v + 16], FREE_STREAM[v]) for v in range(5)]
        change = face_change(inner, outer, side // 2, (-1.0, 1.0)[side % 2])
        for v in range(5):
            lateral[side, 16 * v:16 * v + 16] = change[v]
    lowest, highest = layer == 0, layer == layers - 1
    for way in (0, 1):
        inner = [sendv[way, 16 * v:16 * v + 16] for v in range(5)]
        outer = []
        for v in range(5):
            got = recvv[1 - way, 16 * v:16 * v + 16]
            if way == 0:
                outer.append(jnp.where(lowest, -inner[v] if v == 3 else inner[v], got))
            else:
                outer.append(jnp.where(highest, jnp.full_like(got, FREE_STREAM[v]), got))
        change = face_change(inner, outer, 2, (-1.0, 1.0)[way])
        for v in range(5):
            vertical[way, 16 * v:16 * v + 16] = change[v]


def finish_kernel(cv, acc, lateral, vertical, picks, adv, new, adv_v, new_v, add, out_sem):
    lane_z = lax.broadcasted_iota(jnp.int32, (80, 8, 128), 2) // SLOTS
    sub_z = lax.broadcasted_iota(jnp.int32, (80, 8, 128), 1)
    sub = lax.broadcasted_iota(jnp.int32, (8, 256), 0)
    for side in (2, 3, 0, 1):
        spread = jnp.where(lane_z == sub_z, lateral[side][:, None, :], 0.0).reshape(640, 128)
        hi, lo = split(spread)
        both = jnp.concatenate([hi, lo], axis=1)
        twice = jnp.concatenate([picks[side], picks[side]], axis=0)
        add[side] = dot(both, twice).reshape(5, 4, 32, 256)
    outs = []
    for i in (1, 2, 0, 3):
        for v in range(5):
            for j in range(4):
                for k in range(4):
                    rows_k = pl.ds(8 * k, 8)
                    total = acc[v, i, j, rows_k, :]
                    if i in (0, 3):
                        total = total + add[0 if i == 0 else 1, v, j, rows_k, :]
                    if j in (0, 3):
                        total = total + add[2 if j == 0 else 3, v, i, rows_k, :]
                    m = v * 16 + i * 4 + j
                    if k == 0:
                        total = total + jnp.where(sub == 0, vertical[0, m:m + 1, :], 0.0)
                    if k == 3:
                        total = total + jnp.where(sub == 7, vertical[1, m:m + 1, :], 0.0)
                    new_v[v, i, j, rows_k, :] = total
                    adv_v[v, i, j, rows_k, :] = cv[v, i, j, rows_k, :] + SECTION_WEIGHT * total
        for n, (src, dst) in enumerate(((adv_v, adv), (new_v, new))):
            copy = pltpu.make_async_copy(src.at[:, i], dst.at[:, i], out_sem.at[n, i])
            copy.start()
            outs.append(copy)
    for copy in outs:
        copy.wait()


SHAPE = (5, 4, 4, 32, 256)


def per_device(conserved, register, neighbour, side_type):
    inputs = [
        pltpu.with_memory_space_constraint(x, pltpu.HBM)
        for x in (conserved.reshape(SHAPE), register.reshape(SHAPE), neighbour, side_type)
    ]
    handed = pl.pallas_call(
        exchange_kernel,
        name="exchange",
        out_shape=(
            pltpu.VMEM(SHAPE, F32),
            pltpu.VMEM(SHAPE, F32),
            pltpu.VMEM((4, 80, 128), F32),
            pltpu.VMEM((2, 80, 256), F32),
            pltpu.VMEM((4, 128, 256), BF16),
        ),
        in_specs=[pl.BlockSpec(memory_space=pltpu.HBM)] * 4,
        out_specs=tuple([pl.BlockSpec(memory_space=pltpu.VMEM)] * 5),
        scratch_shapes=[
            pltpu.VMEM((4, 256), jnp.int32),
            pltpu.VMEM((4, 256), jnp.int32),
            pltpu.VMEM(SHAPE, F32),
            pltpu.VMEM((5, 4, 32, 256), F32),
            pltpu.VMEM((4, 640, 128), F32),
            pltpu.VMEM((4, 80, 128), F32),
            pltpu.VMEM((4, 88, 128), F32),
            pltpu.VMEM((4, 80, 128), F32),
            pltpu.VMEM((2, 80, 256), F32),
            pltpu.VMEM((2, 80, 256), F32),
            pltpu.SemaphoreType.DMA((8,)),
            pltpu.SemaphoreType.DMA((4,)),
            pltpu.SemaphoreType.DMA((4,)),
            pltpu.SemaphoreType.DMA((2,)),
            pltpu.SemaphoreType.DMA((2,)),
        ],
        compiler_params=pltpu.CompilerParams(
            collective_id=0, has_side_effects=True, vmem_limit_bytes=40 * 1024 * 1024
        ),
    )(*inputs)
    handed = [pltpu.with_memory_space_constraint(x, pltpu.VMEM) for x in handed]
    adv, new = pl.pallas_call(
        finish_kernel,
        name="finish",
        out_shape=(jax.ShapeDtypeStruct(SHAPE, F32), jax.ShapeDtypeStruct(SHAPE, F32)),
        in_specs=[pl.BlockSpec(memory_space=pltpu.VMEM)] * 5,
        out_specs=(pl.BlockSpec(memory_space=pltpu.HBM), pl.BlockSpec(memory_space=pltpu.HBM)),
        scratch_shapes=[
            pltpu.VMEM(SHAPE, F32),
            pltpu.VMEM(SHAPE, F32),
            pltpu.VMEM((4, 5, 4, 32, 256), F32),
            pltpu.SemaphoreType.DMA((2, 4)),
        ],
        compiler_params=pltpu.CompilerParams(vmem_limit_bytes=32 * 1024 * 1024),
    )(*handed)
    full = (5, 4, 4, 4, 8, 256)
    return adv.reshape(full), new.reshape(full)


def solution(mesh):
    spec = P(None, None, None, None, "layer", "foot")
    return jax.shard_map(
        per_device,
        mesh=mesh,
        in_specs=(spec, spec, P(None, "foot"), P(None, "foot")),
        out_specs=(spec, spec),
        check_vma=False,
    )
```

time: 24.4 us -> 20.7 us (0.85)
  local copies, waits for them, and re-layouts: 4.16 us -> 0 us
  Pallas kernels: 19.4 us -> 20 us
    unnamed x8 -> x0, local copies, waits for them, and re-layouts: 4.16 us -> none
    pallas_call x2, Pallas kernels: 19.4 us -> 20 us  [the longest x1 16.8 us: per_device(): pl.pallas_call(exchange_kernel, name='exchange', out_shape=(pltpu.VMEM(SH...]
where the time goes in v2:
time: 20.7 us; the launch traced here: 20.6 us
  Pallas kernels  20 us (97%)
  between operations  0.64 us (3%)
    pallas_call x1, Pallas kernels, per_device(): pl.pallas_call(exchange_kernel, name='exchange', out_shape=(pltpu.VMEM(SH...  16.8 us
    pallas_call x1, Pallas kernels, per_device(): pl.pallas_call(finish_kernel, name='finish', out_shape=(jax.ShapeDtypeStr...  3.19 us

profile of v2, /device:TPU:1, one launch (start us, length us, event | category | flops | bytes accessed | tf_op | source)
XLA Modules:
  0.0 20.6 jit_solution(5610115505641271076)
XLA Ops:
  0.6 16.8 %exchange.1 = (f32[5,4,4,32,256]{4,3,2,1,0:T(8,128)S(1)}, f32[5,4,4,32,256]{4,3,2,1,0:T(8,128)S(1)}, f32[4,80,128]{2,1,0:T(8,128)S(1)}, f32[2,80,256]{2,1,0:T(8,128)S(1)}, bf16[4,128,256]{2,1,0:T(8,128)(2,1)S(1)}) custom-call(f32[5,4,4,32,256]{4,3,2,1,0:T(8,128)} %bitcast.4, f32[5,4,4,32,256]{4,3,2,1,0:T(8,128)} %bitcast.5, s32[4,256]{1,0:T(4,128)} %nb_in.1, ...), custom_call_target="tpu_custom_call" | custom-call | tf_op jit(solution)/shard_map/exchange/pallas_call | solution.py:370
  17.4 3.2 %finish.1 = (f32[5,4,4,32,256]{4,3,2,1,0:T(8,128)}, f32[5,4,4,32,256]{4,3,2,1,0:T(8,128)}) custom-call(f32[5,4,4,32,256]{4,3,2,1,0:T(8,128)S(1)} %get-tuple-element.9.cv, f32[5,4,4,32,256]{4,3,2,1,0:T(8,128)S(1)} %get-tuple-element.10.acc, f32[4,80,128]{2,1,0:T(8,128)S(1)} %get-tuple-element.11.lateral, f32[2,80,256]{2,1,0:T(8,128)S(1)} %get-tuple-element.12.vertical, ...), custom_call_target="tpu_custom_call" | custom-call | tf_op jit(solution)/shard_map/finish/pallas_call | solution.py:404

commit v3 on v2

--- a/solution.py
+++ b/solution.py
@@ -113,7 +113,7 @@
 
 def exchange_kernel(
     cons, reg, nb_in, kinds_in, cv, acc, lateral, vertical, picks,
-    nb, kinds, prim, ghost, stage, packed, own, arrived, sendv, recvv, load_sem, send_sem, recv_sem, vsend_sem, vrecv_sem,
+    nb, kinds, regv, prim, ghost, stage, packed, own, arrived, sendv, recvv, load_sem, send_sem, recv_sem, vsend_sem, vrecv_sem,
 ):
     foot, layer = lax.axis_index("foot"), lax.axis_index("layer")
     feet, layers = lax.axis_size("foot"), lax.axis_size("layer")
@@ -137,7 +137,7 @@
     loads = [pltpu.make_async_copy(cons.at[v], cv.at[v], load_sem.at[v]) for v in range(5)]
     for copy in loads:
         copy.start()
-    reg_load = pltpu.make_async_copy(reg, acc, load_sem.at[5])
+    reg_load = pltpu.make_async_copy(reg, regv, load_sem.at[5])
     reg_load.start()
 
     slot = lax.bitwise_and(lax.broadcasted_iota(jnp.int32, (128, 256), 0), SLOTS - 1)
@@ -150,7 +150,17 @@
     here = nb[...] - foot * 256
     mask = jnp.where(jnp.logical_or(here < 0, here >= 256), 1.0, 0.0)
     mask8 = jnp.concatenate([mask, jnp.zeros_like(mask)], axis=0).astype(BF16)
-    rank = jnp.where(mask8.astype(F32) > 0.5, dot(mask8, before), -1.0).astype(jnp.int32)
+    away = mask > 0.5
+    rank = jnp.where(away, dot(mask8, before)[0:4], -1.0).astype(jnp.int32)
+    names = jnp.where(away, lax.bitwise_and(nb[...], 255), 1000).astype(F32)
+    names_down = jnp.transpose(jnp.concatenate([names, names], axis=0))
+    kind = kinds[...]
+    open_face = kind == 0
+    orders = []
+    for side in range(4):
+        less = jnp.where(names_down[:, side:side + 1] < names[side:side + 1], 1.0, 0.0)
+        order = jnp.sum(less, axis=0, keepdims=True)
+        orders.append(jnp.where(jnp.logical_and(open_face, away)[side:side + 1], order, -1.0).astype(jnp.int32))
 
     for copy in loads:
         copy.wait()
@@ -161,28 +171,17 @@
             stage[2 * way + h] = cv[:, :, :, pl.ds(24 * way, 8), lanes].reshape(640, 128)
             sendv[way, :, lanes] = stage[2 * way + h, pl.ds(7 * way, 80, stride=8), :]
     for side in range(4):
-        hi, lo = split(trace_of(cv, side ^ 1))
-        pick = jnp.where(rank[(side ^ 1):(side ^ 1) + 1] == slot, 1.0, 0.0).astype(BF16)
-        stage[side] = dot_nt(hi, pick) + dot_nt(lo, pick)
-        packed[side] = gather_slots(stage, side, lane_z)
-
-    pl.semaphore_wait(barrier, len(partners))
-    copies = []
-    for side in range(4):
-        copies.append(pltpu.make_async_remote_copy(
-            src_ref=packed.at[side], dst_ref=arrived.at[side], send_sem=send_sem.at[side],
-            recv_sem=recv_sem.at[side], device_id=at_foot(STEPS[side]), device_id_type=MESH,
-        ))
-    for way in (0, 1):
-        copies.append(pltpu.make_async_remote_copy(
-            src_ref=sendv.at[way], dst_ref=recvv.at[way], send_sem=vsend_sem.at[way],
-            recv_sem=vrecv_sem.at[way], device_id=at_layer((-1, 1)[way]), device_id_type=MESH,
-        ))
-    for copy in copies:
-        copy.start()
-
-    reg_load.wait()
-
+        hi, lo = split(trace_of(cv, side))
+        send = jnp.where(rank[side:side + 1] == slot, 1.0, 0.0).astype(BF16)
+        pick = jnp.where(orders[side] == slot, 1.0, 0.0).astype(BF16)
+        picks[side] = pick
+        both = jnp.concatenate([send, pick], axis=0)
+        rows_both = dot_nt(hi, both) + dot_nt(lo, both)
+        stage[0] = rows_both[:, :128]
+        stage[1] = rows_both[:, 128:]
+        packed[side ^ 1] = gather_slots(stage, 0, lane_z)
+        own[side, 0:80] = gather_slots(stage, 1, lane_z)
+        own[side, 80:88] = dot_nt(jnp.ones((8, 256), BF16), pick)
     def z_lines(line, carry):
         i, j = line // 4, line % 4
         q = [[cv[v, i, j, pl.ds(8 * k, 8), :] for k in range(4)] for v in range(5)]
@@ -206,10 +205,27 @@
             out = derived(flux[v])
             for k in range(4):
                 rows_k = pl.ds(8 * k, 8)
-                acc[v, i, j, rows_k, :] = SECTION_DECAY * acc[v, i, j, rows_k, :] + out[k]
+                acc[v, i, j, rows_k, :] = out[k]
         return carry
 
     lax.fori_loop(0, 16, z_lines, 0)
+
+
+    pl.semaphore_wait(barrier, len(partners))
+    copies = []
+    for side in range(4):
+        copies.append(pltpu.make_async_remote_copy(
+            src_ref=packed.at[side], dst_ref=arrived.at[side], send_sem=send_sem.at[side],
+            recv_sem=recv_sem.at[side], device_id=at_foot(STEPS[side]), device_id_type=MESH,
+        ))
+    for way in (0, 1):
+        copies.append(pltpu.make_async_remote_copy(
+            src_ref=sendv.at[way], dst_ref=recvv.at[way], send_sem=vsend_sem.at[way],
+            recv_sem=vrecv_sem.at[way], device_id=at_layer((-1, 1)[way]), device_id_type=MESH,
+        ))
+    for copy in copies:
+        copy.start()
+
 
     def lines(direction, line, carry):
         a, k = line // 4, line % 4
@@ -233,14 +249,15 @@
         for v in range(5):
             out = derived(flux[v])
             for node in range(4):
-                acc[(v,) + at(node)] = acc[(v,) + at(node)] + out[node]
+                total = acc[(v,) + at(node)] + out[node]
+                if direction == 1:
+                    total = total + SECTION_DECAY * regv[(v,) + at(node)]
+                acc[(v,) + at(node)] = total
         return carry
 
     lax.fori_loop(0, 16, functools.partial(lines, 0), 0)
+    reg_load.wait()
     lax.fori_loop(0, 16, functools.partial(lines, 1), 0)
-
-    kind = kinds[...]
-    open_face = kind == 0
     for side in range(4):
         hi, lo = split(trace_of(cv, side ^ 1))
         select = jnp.where(here[side:side + 1] == rows, 1.0, 0.0).astype(BF16)
@@ -265,20 +282,7 @@
                 acc[(v,) + at] = acc[(v,) + at] + change[v]
             return carry
 
-        lax.fori_loop(0, 16, lateral_nodes, 0, unroll=2)
-
-        named = lax.bitwise_and(nb[side:side + 1], 255)
-        named = jnp.where(mask[side:side + 1] > 0.5, named, -1)
-        onehot = jnp.where(rows == named, 1.0, 0.0).astype(BF16)
-        hit = dot_nt(jnp.ones((8, 256), BF16), onehot).astype(BF16)
-        order = dot(dot(hit, before).astype(BF16), onehot)
-        order = jnp.where(jnp.logical_and(open_face, mask > 0.5)[side:side + 1], order[0:1], -1.0)
-        pick = jnp.where(order.astype(jnp.int32) == slot, 1.0, 0.0).astype(BF16)
-        picks[side] = pick
-        hi, lo = split(trace_of(cv, side))
-        stage[side] = dot_nt(hi, pick) + dot_nt(lo, pick)
-        own[side, 0:80] = gather_slots(stage, side, lane_z)
-        own[side, 80:88] = dot_nt(jnp.ones((8, 256), BF16), pick)
+        lax.fori_loop(0, 16, lateral_nodes, 0, unroll=4)
 
     sub = lax.broadcasted_iota(jnp.int32, (8, 256), 0)
     for way in (0, 1):
@@ -296,7 +300,7 @@
                 acc[(v,) + at] = acc[(v,) + at] + change[v]
             return carry
 
-        lax.fori_loop(0, 16, vertical_nodes, 0, unroll=2)
+        lax.fori_loop(0, 16, vertical_nodes, 0, unroll=4)
 
     for copy in copies:
         copy.wait()
@@ -321,20 +325,23 @@
         change = face_change(inner, outer, 2, (-1.0, 1.0)[way])
         for v in range(5):
             vertical[way, 16 * v:16 * v + 16] = change[v]
-
-
 def finish_kernel(cv, acc, lateral, vertical, picks, adv, new, adv_v, new_v, add, out_sem):
     lane_z = lax.broadcasted_iota(jnp.int32, (80, 8, 128), 2) // SLOTS
     sub_z = lax.broadcasted_iota(jnp.int32, (80, 8, 128), 1)
     sub = lax.broadcasted_iota(jnp.int32, (8, 256), 0)
-    for side in (2, 3, 0, 1):
+    def unpack(side):
         spread = jnp.where(lane_z == sub_z, lateral[side][:, None, :], 0.0).reshape(640, 128)
         hi, lo = split(spread)
         both = jnp.concatenate([hi, lo], axis=1)
         twice = jnp.concatenate([picks[side], picks[side]], axis=0)
         add[side] = dot(both, twice).reshape(5, 4, 32, 256)
+
     outs = []
+    unpack(2)
+    unpack(3)
     for i in (1, 2, 0, 3):
+        if i in (0, 3):
+            unpack(0 if i == 0 else 1)
         for v in range(5):
             for j in range(4):
                 for k in range(4):
@@ -382,6 +389,7 @@
         scratch_shapes=[
             pltpu.VMEM((4, 256), jnp.int32),
             pltpu.VMEM((4, 256), jnp.int32),
+            pltpu.VMEM(SHAPE, F32),
             pltpu.VMEM(SHAPE, F32),
             pltpu.VMEM((5, 4, 32, 256), F32),
             pltpu.VMEM((4, 640, 128), F32),

time: 20.7 us -> 19.1 us (0.923)
  Pallas kernels: 20 us -> 18.4 us
    pallas_call x1, Pallas kernels: 16.8 us -> 15.2 us  [per_device(): pl.pallas_call(exchange_kernel, name='exchange', out_shape=(pltpu.VMEM(SH...]
where the time goes in v3:
time: 19.1 us; the launch traced here: 19 us
  Pallas kernels  18.4 us (96%)
  between operations  0.64 us (3%)
    pallas_call x1, Pallas kernels, per_device(): pl.pallas_call(exchange_kernel, name='exchange', out_shape=(pltpu.VMEM(SH...  15.2 us
    pallas_call x1, Pallas kernels, per_device(): pl.pallas_call(finish_kernel, name='finish', out_shape=(jax.ShapeDtypeStr...  3.18 us

profile of v3, /device:TPU:1, one launch (start us, length us, event | category | flops | bytes accessed | tf_op | source)
XLA Modules:
  0.0 19.0 jit_solution(5818735952247601586)
XLA Ops:
  0.6 15.2 %exchange.1 = (f32[5,4,4,32,256]{4,3,2,1,0:T(8,128)S(1)}, f32[5,4,4,32,256]{4,3,2,1,0:T(8,128)S(1)}, f32[4,80,128]{2,1,0:T(8,128)S(1)}, f32[2,80,256]{2,1,0:T(8,128)S(1)}, bf16[4,128,256]{2,1,0:T(8,128)(2,1)S(1)}) custom-call(f32[5,4,4,32,256]{4,3,2,1,0:T(8,128)} %bitcast.4, f32[5,4,4,32,256]{4,3,2,1,0:T(8,128)} %bitcast.5, s32[4,256]{1,0:T(4,128)} %nb_in.1, ...), custom_call_target="tpu_custom_call" | custom-call | tf_op jit(solution)/shard_map/exchange/pallas_call | solution.py:377
  15.8 3.2 %finish.1 = (f32[5,4,4,32,256]{4,3,2,1,0:T(8,128)}, f32[5,4,4,32,256]{4,3,2,1,0:T(8,128)}) custom-call(f32[5,4,4,32,256]{4,3,2,1,0:T(8,128)S(1)} %get-tuple-element.9.cv, f32[5,4,4,32,256]{4,3,2,1,0:T(8,128)S(1)} %get-tuple-element.10.acc, f32[4,80,128]{2,1,0:T(8,128)S(1)} %get-tuple-element.11.lateral, f32[2,80,256]{2,1,0:T(8,128)S(1)} %get-tuple-element.12.vertical, ...), custom_call_target="tpu_custom_call" | custom-call | tf_op jit(solution)/shard_map/finish/pallas_call | solution.py:412

commit v4 on v1

--- a/solution.py
+++ b/solution.py
@@ -17,7 +17,7 @@
 SLOTS = 16
 BF16 = jnp.bfloat16
 F32 = jnp.float32
-STEPS = (4, -4, 1, -1)
+TILES_Y = 4
 
 
 def derivative_entries():
@@ -70,88 +70,114 @@
     return lax.dot_general(a, b, (((1,), (1,)), ((), ())), preferred_element_type=F32)
 
 
+def face_rows(side):
+    face = (0, 3)[side % 2]
+    return (slice(None), face) if side < 2 else (slice(None), slice(None), face)
+
+
 def trace_of(cv, side):
-    face = (0, 3)[side % 2]
-    block = cv[:, face] if side < 2 else cv[:, :, face]
-    return block.reshape(640, 256)
+    return cv[face_rows(side)].reshape(640, 256)
+
+
+def primitive(q):
+    r = inverse(q[0])
+    kinetic = (q[1] * q[1] + q[2] * q[2] + q[3] * q[3]) * r
+    pressure = 0.4 * q[4] - 0.2 * kinetic
+    square = 1.4 * pressure * r
+    return r, pressure, square * lax.rsqrt(square)
+
+
+def gather_slots(stage, side, lane_z):
+    total = stage[side, pl.ds(0, 80, stride=8), :]
+    for z in range(1, 8):
+        total = jnp.where(lane_z == z, stage[side, pl.ds(z, 80, stride=8), :], total)
+    return total
 
 
 def exchange_kernel(
-    cons, reg, nb, cv, acc, ghost, vert,
-    prim, stage, packed, arrived, sendv, recvv, load_sem, send_sem, recv_sem, vsend_sem, vrecv_sem,
+    cons, reg, nb_in, cv, acc, ghost, vert,
+    nb, regv, prim, halves, picks, stage, packed, arrived, sendv, recvv,
+    load_sem, send_sem, recv_sem, vsend_sem, vrecv_sem,
 ):
     foot, layer = lax.axis_index("foot"), lax.axis_index("layer")
-    feet, layers = lax.axis_size("foot"), lax.axis_size("layer")
-
-    def at_foot(by):
-        return (lax.rem(foot + by + feet, feet), layer)
-
-    def at_layer(by):
-        return (foot, lax.rem(layer + by + layers, layers))
-
+    layers = lax.axis_size("layer")
+    along, across = foot // TILES_Y, lax.rem(foot, TILES_Y)
+    tiles = lax.axis_size("foot") // TILES_Y
+
+    lower, upper = along > 0, along < tiles - 1
+    left, right = across > 0, across < TILES_Y - 1
+    below, above = layer > 0, layer < layers - 1
+    sends = [
+        ((foot + TILES_Y, layer), upper, lower),
+        ((foot - TILES_Y, layer), lower, upper),
+        ((foot + 1, layer), right, left),
+        ((foot - 1, layer), left, right),
+        ((foot, layer - 1), below, above),
+        ((foot, layer + 1), above, below),
+    ]
+
+    barrier = pltpu.get_barrier_semaphore()
+    partners = jnp.int32(0)
+    for partner, there, _ in sends:
+        partners = partners + there.astype(jnp.int32)
+
+        @pl.when(there)
+        def _():
+            pl.semaphore_signal(barrier, inc=1, device_id=partner, device_id_type=MESH)
+
+    nb_load = pltpu.make_async_copy(nb_in, nb, load_sem.at[6])
+    nb_load.start()
     loads = [pltpu.make_async_copy(cons.at[v], cv.at[v], load_sem.at[v]) for v in range(5)]
     for copy in loads:
         copy.start()
-    reg_load = pltpu.make_async_copy(reg, acc, load_sem.at[5])
+    reg_load = pltpu.make_async_copy(reg, regv, load_sem.at[5])
     reg_load.start()
 
-    barrier = pltpu.get_barrier_semaphore()
-    partners = [at_foot(by) for by in STEPS] + [at_layer(by) for by in (1, -1)]
-    for partner in partners:
-        pl.semaphore_signal(barrier, inc=1, device_id=partner, device_id_type=MESH)
-
-    here = nb[...] - foot * 256
-    remote = jnp.logical_or(here < 0, here >= 256)
-    mask = jnp.where(remote, 1.0, 0.0)
-    mask8 = jnp.concatenate([mask, jnp.zeros_like(mask)], axis=0).astype(BF16)
+    slot = lax.bitwise_and(lax.broadcasted_iota(jnp.int32, (128, 256), 0), SLOTS - 1)
+    lane_z = lax.broadcasted_iota(jnp.int32, (80, 128), 1) // SLOTS
     rows = lax.broadcasted_iota(jnp.int32, (256, 256), 0)
     cols = lax.broadcasted_iota(jnp.int32, (256, 256), 1)
     before = jnp.where(rows < cols, 1.0, 0.0).astype(BF16)
-    rank = dot(mask8, before)
-    rank = jnp.where(mask8.astype(F32) > 0.5, rank, -1.0).astype(jnp.int32)
-    named = (lax.bitwise_and(nb[...], 255) + 1).astype(F32)
-    named8 = jnp.concatenate([named, jnp.zeros_like(named)], axis=0).astype(BF16)
-    slot = lax.bitwise_and(lax.broadcasted_iota(jnp.int32, (128, 256), 0), SLOTS - 1)
-    lane_z = lax.broadcasted_iota(jnp.int32, (80, 128), 1) // SLOTS
+    nb_load.wait()
+    here = nb[...] - foot * 256
+    away = jnp.logical_or(here < 0, here >= 256)
+    mask = jnp.where(away, 1.0, 0.0)
+    mask8 = jnp.concatenate([mask, jnp.zeros_like(mask)], axis=0).astype(BF16)
+    rank = jnp.where(away, dot(mask8, before)[0:4], -1.0).astype(jnp.int32)
 
     for copy in loads:
         copy.wait()
-    pl.semaphore_wait(barrier, len(partners))
-
-    vcopies = []
+
     for way in (0, 1):
         for h in (0, 1):
             lanes = pl.ds(h * 128, 128)
             stage[2 * way + h] = cv[:, :, :, pl.ds(24 * way, 8), lanes].reshape(640, 128)
             sendv[way, :, lanes] = stage[2 * way + h, pl.ds(7 * way, 80, stride=8), :]
-        copy = pltpu.make_async_remote_copy(
-            src_ref=sendv.at[way], dst_ref=recvv.at[way], send_sem=vsend_sem.at[way],
-            recv_sem=vrecv_sem.at[way], device_id=at_layer((-1, 1)[way]), device_id_type=MESH,
-        )
-        copy.start()
-        vcopies.append(copy)
-
+    for side in range(4):
+        hi, lo = split(trace_of(cv, side))
+        halves[side, :, 0:256] = hi
+        halves[side, :, 256:512] = lo
+        send = jnp.where(rank[side:side + 1] == slot, 1.0, 0.0).astype(BF16)
+        stage[side] = dot_nt(hi, send) + dot_nt(lo, send)
+        packed[side ^ 1] = gather_slots(stage, side, lane_z)
+
+    pl.semaphore_wait(barrier, partners)
     copies = []
     for side in range(4):
-        q = side ^ 1
-        hi, lo = split(trace_of(cv, q))
-        pick = jnp.where(rank[q:q + 1] == slot, 1.0, 0.0).astype(BF16)
-        stage[side] = dot_nt(hi, pick) + dot_nt(lo, pick)
-        total = stage[side, pl.ds(0, 80, stride=8), :]
-        for z in range(1, 8):
-            total = jnp.where(lane_z == z, stage[side, pl.ds(z, 80, stride=8), :], total)
-        packed[side, 0:80] = total
-        packed[side, 80:88] = dot_nt(named8, pick)
-        copy = pltpu.make_async_remote_copy(
+        copies.append(pltpu.make_async_remote_copy(
             src_ref=packed.at[side], dst_ref=arrived.at[side], send_sem=send_sem.at[side],
-            recv_sem=recv_sem.at[side], device_id=at_foot(STEPS[side]), device_id_type=MESH,
-        )
-        copy.start()
-        copies.append(copy)
-        select = jnp.where(here[side:side + 1] == rows, 1.0, 0.0).astype(BF16)
-        ghost[side] = (dot(hi, select) + dot(lo, select)).reshape(5, 4, 32, 256)
-
-    reg_load.wait()
+            recv_sem=recv_sem.at[side], device_id=sends[side][0], device_id_type=MESH,
+        ))
+    for way in (0, 1):
+        copies.append(pltpu.make_async_remote_copy(
+            src_ref=sendv.at[way], dst_ref=recvv.at[way], send_sem=vsend_sem.at[way],
+            recv_sem=vrecv_sem.at[way], device_id=sends[4 + way][0], device_id_type=MESH,
+        ))
+    for copy, (_, there, _) in zip(copies, sends):
+
+        @pl.when(there)
+        def _():
+            copy.start()
 
     def z_lines(line, carry):
         i, j = line // 4, line % 4
@@ -160,8 +186,7 @@
         for k in range(4):
             rho, mx, my, mz, energy = (q[v][k] for v in range(5))
             r = inverse(rho)
-            kinetic = (mx * mx + my * my + mz * mz) * r
-            pressure = 0.4 * energy - 0.2 * kinetic
+            pressure = 0.4 * energy - 0.2 * ((mx * mx + my * my + mz * mz) * r)
             vz = mz * r
             rows_k = pl.ds(8 * k, 8)
             prim[0, i, j, rows_k, :] = mx * r
@@ -176,10 +201,11 @@
             out = derived(flux[v])
             for k in range(4):
                 rows_k = pl.ds(8 * k, 8)
-                acc[v, i, j, rows_k, :] = SECTION_DECAY * acc[v, i, j, rows_k, :] + out[k]
+                acc[v, i, j, rows_k, :] = out[k]
         return carry
 
     lax.fori_loop(0, 16, z_lines, 0)
+
 
     def lines(direction, line, carry):
         a, k = line // 4, line % 4
@@ -203,43 +229,68 @@
         for v in range(5):
             out = derived(flux[v])
             for node in range(4):
-                acc[(v,) + at(node)] = acc[(v,) + at(node)] + out[node]
+                total = acc[(v,) + at(node)] + out[node]
+                if direction == 1:
+                    total = total + SECTION_DECAY * regv[(v,) + at(node)]
+                acc[(v,) + at(node)] = total
         return carry
 
     lax.fori_loop(0, 16, functools.partial(lines, 0), 0)
+    reg_load.wait()
     lax.fori_loop(0, 16, functools.partial(lines, 1), 0)
+
+    names = jnp.where(away, lax.bitwise_and(nb[...], 255), 1000).astype(F32)
+    names_down = jnp.transpose(jnp.concatenate([names, names], axis=0))
+    for side in range(4):
+        less = jnp.where(names_down[:, side:side + 1] < names[side:side + 1], 1.0, 0.0)
+        order = jnp.sum(less, axis=0, keepdims=True)
+        order = jnp.where(away[side:side + 1], order, -1.0).astype(jnp.int32)
+        picks[side] = jnp.where(order == slot, 1.0, 0.0).astype(BF16)
 
     lane_z3 = lax.broadcasted_iota(jnp.int32, (80, 8, 128), 2) // SLOTS
     sub_z3 = lax.broadcasted_iota(jnp.int32, (80, 8, 128), 1)
-    column = (lax.broadcasted_iota(jnp.int32, (256, 128), 0) + 1).astype(F32)
     for side in range(4):
-        copies[side].wait()
-        q = side ^ 1
-        place = jnp.where(arrived[side, 80 + q:81 + q] == column, 1.0, 0.0).astype(BF16)
-        spread = jnp.where(lane_z3 == sub_z3, arrived[side, 0:80][:, None, :], 0.0).reshape(640, 128)
-        hi, lo = split(spread)
-        both = jnp.concatenate([hi, lo], axis=1)
-        twice = jnp.concatenate([place, place], axis=1)
-        ghost[side] = ghost[side] + dot_nt(both, twice).reshape(5, 4, 32, 256)
-
-    for copy in vcopies:
-        copy.wait()
-    lowest, highest = layer == 0, layer == layers - 1
+        _, there, comes = sends[side]
+
+        @pl.when(there)
+        def _():
+            copies[side].wait_send()
+
+        @pl.when(comes)
+        def _():
+            copies[side].wait_recv()
+
+        @pl.when(jnp.logical_not(comes))
+        def _():
+            arrived[side] = jnp.zeros((80, 128), F32)
+
+        spread = jnp.where(lane_z3 == sub_z3, arrived[side][:, None, :], 0.0).reshape(640, 128)
+        far_hi, far_lo = split(spread)
+        select = jnp.where(here[side:side + 1] == rows, 1.0, 0.0).astype(BF16)
+        left_side = jnp.concatenate([halves[side ^ 1], far_hi, far_lo], axis=1)
+        right_side = jnp.concatenate([select, select, picks[side], picks[side]], axis=0)
+        ghost[side] = dot(left_side, right_side).reshape(5, 4, 32, 256)
+
+    for way in (0, 1):
+        _, there, comes = sends[4 + way]
+
+        @pl.when(there)
+        def _():
+            copies[4 + way].wait_send()
+
+        @pl.when(comes)
+        def _():
+            copies[4 + way].wait_recv()
+
+        @pl.when(jnp.logical_not(comes))
+        def _():
+            recvv[way] = jnp.zeros((80, 256), F32)
+
     for v in range(5):
         part = pl.ds(16 * v, 16)
         own = sendv[0, part, :]
-        vert[0, part, :] = jnp.where(lowest, -own if v == 3 else own, recvv[1, part, :])
-        vert[1, part, :] = jnp.where(highest, jnp.full_like(own, FREE_STREAM[v]), recvv[0, part, :])
-
-
-def state(q, direction, need_all=False):
-    rho, energy = q[0], q[4]
-    r = inverse(rho)
-    kinetic = (q[1] * q[1] + q[2] * q[2] + q[3] * q[3]) * r
-    pressure = 0.4 * energy - 0.2 * kinetic
-    square = 1.4 * pressure * r
-    sound = square * lax.rsqrt(square)
-    return r, pressure, sound
+        vert[0, part, :] = jnp.where(below, recvv[1, part, :], -own if v == 3 else own)
+        vert[1, part, :] = jnp.where(above, recvv[0, part, :], jnp.full_like(own, FREE_STREAM[v]))
 
 
 def surface_kernel(cv, acc, ghost, vert, kinds, adv, new, adv_v, new_v, out_sem):
@@ -265,7 +316,7 @@
                     if k in (0, 3):
                         faces.append((2, 4 if k == 0 else 5, (i, j)))
                     if faces:
-                        r_in, p_in, c_in = state(q, 0)
+                        r_in, p_in, c_in = primitive(q)
                     for d, side, (a, b) in faces:
                         if side < 4:
                             outer = []
@@ -289,7 +340,7 @@
                                     edge = jnp.broadcast_to(vert[1, m:m + 1, lanes], (8, 128))
                                     outer.append(jnp.where(sub == 7, edge, near))
                         sign = -1.0 if side % 2 == 0 else 1.0
-                        r_out, p_out, c_out = state(outer, d)
+                        r_out, p_out, c_out = primitive(outer)
                         v_in, v_out = q[1 + d] * r_in, outer[1 + d] * r_out
                         lam = LIFT * jnp.maximum(jnp.abs(v_in) + c_in, jnp.abs(v_out) + c_out)
                         s_in, s_out = (sign * LIFT) * v_in, (sign * LIFT) * v_out
@@ -312,32 +363,37 @@
         copy.wait()
 
 
+SHAPE = (5, 4, 4, 32, 256)
+
+
 def per_device(conserved, register, neighbour, side_type):
-    shape = (5, 4, 4, 32, 256)
-    cons, reg = conserved.reshape(shape), register.reshape(shape)
-    cv, acc, ghost, vert = pl.pallas_call(
+    inputs = [
+        pltpu.with_memory_space_constraint(x, pltpu.HBM)
+        for x in (conserved.reshape(SHAPE), register.reshape(SHAPE), neighbour)
+    ]
+    handed = pl.pallas_call(
         exchange_kernel,
         name="exchange",
         out_shape=(
-            pltpu.VMEM(shape, F32),
-            pltpu.VMEM(shape, F32),
+            pltpu.VMEM(SHAPE, F32),
+            pltpu.VMEM(SHAPE, F32),
             pltpu.VMEM((4, 5, 4, 32, 256), F32),
             pltpu.VMEM((2, 80, 256), F32),
         ),
-        in_specs=[
-            pl.BlockSpec(memory_space=pl.ANY),
-            pl.BlockSpec(memory_space=pl.ANY),
-            pl.BlockSpec(memory_space=pltpu.VMEM),
-        ],
+        in_specs=[pl.BlockSpec(memory_space=pltpu.HBM)] * 3,
         out_specs=tuple([pl.BlockSpec(memory_space=pltpu.VMEM)] * 4),
         scratch_shapes=[
+            pltpu.VMEM((4, 256), jnp.int32),
+            pltpu.VMEM(SHAPE, F32),
             pltpu.VMEM((3, 4, 4, 32, 256), F32),
+            pltpu.VMEM((4, 640, 512), BF16),
+            pltpu.VMEM((4, 128, 256), BF16),
             pltpu.VMEM((4, 640, 128), F32),
-            pltpu.VMEM((4, 88, 128), F32),
-            pltpu.VMEM((4, 88, 128), F32),
+            pltpu.VMEM((4, 80, 128), F32),
+            pltpu.VMEM((4, 80, 128), F32),
             pltpu.VMEM((2, 80, 256), F32),
             pltpu.VMEM((2, 80, 256), F32),
-            pltpu.SemaphoreType.DMA((6,)),
+            pltpu.SemaphoreType.DMA((7,)),
             pltpu.SemaphoreType.DMA((4,)),
             pltpu.SemaphoreType.DMA((4,)),
             pltpu.SemaphoreType.DMA((2,)),
@@ -346,23 +402,21 @@
         compiler_params=pltpu.CompilerParams(
             collective_id=0, has_side_effects=True, vmem_limit_bytes=40 * 1024 * 1024
         ),
-    )(cons, reg, neighbour)
-    cv, acc, ghost, vert = (
-        pltpu.with_memory_space_constraint(x, pltpu.VMEM) for x in (cv, acc, ghost, vert)
-    )
+    )(*inputs)
+    handed = [pltpu.with_memory_space_constraint(x, pltpu.VMEM) for x in handed]
     adv, new = pl.pallas_call(
         surface_kernel,
         name="surface",
-        out_shape=(jax.ShapeDtypeStruct(shape, F32), jax.ShapeDtypeStruct(shape, F32)),
+        out_shape=(jax.ShapeDtypeStruct(SHAPE, F32), jax.ShapeDtypeStruct(SHAPE, F32)),
         in_specs=[pl.BlockSpec(memory_space=pltpu.VMEM)] * 5,
-        out_specs=(pl.BlockSpec(memory_space=pl.ANY), pl.BlockSpec(memory_space=pl.ANY)),
+        out_specs=(pl.BlockSpec(memory_space=pltpu.HBM), pl.BlockSpec(memory_space=pltpu.HBM)),
         scratch_shapes=[
-            pltpu.VMEM(shape, F32),
-            pltpu.VMEM(shape, F32),
+            pltpu.VMEM(SHAPE, F32),
+            pltpu.VMEM(SHAPE, F32),
             pltpu.SemaphoreType.DMA((2, 4)),
         ],
         compiler_params=pltpu.CompilerParams(vmem_limit_bytes=32 * 1024 * 1024),
-    )(cv, acc, ghost, vert, side_type)
+    )(*handed, side_type)
     full = (5, 4, 4, 4, 8, 256)
     return adv.reshape(full), new.reshape(full)
 

time: 24.4 us -> 15.6 us (0.64)
  the two profiles are of different devices: /device:TPU:1 before, /device:TPU:102 now
where the time goes in v4:
time: 15.6 us; the launch traced here: 15.5 us
  Pallas kernels  14.9 us (96%)
  between operations  0.65 us (4%)
    pallas_call x1, Pallas kernels, per_device(): pl.pallas_call(exchange_kernel, name='exchange', out_shape=(pltpu.VMEM(SH...  11.3 us
    pallas_call x1, Pallas kernels, per_device(): pl.pallas_call(surface_kernel, name='surface', out_shape=(jax.ShapeDtypeS...  3.51 us

profile of v4, /device:TPU:102, one launch (start us, length us, event | category | flops | bytes accessed | tf_op | source)
XLA Modules:
  0.0 15.5 jit_solution(3003717833668808466)
XLA Ops:
  0.6 0.0 copy-start
  0.6 11.3 %exchange.1 = (f32[5,4,4,32,256]{4,3,2,1,0:T(8,128)S(1)}, f32[5,4,4,32,256]{4,3,2,1,0:T(8,128)S(1)}, f32[4,5,4,32,256]{4,3,2,1,0:T(8,128)S(1)}, f32[2,80,256]{2,1,0:T(8,128)S(1)}) custom-call(f32[5,4,4,32,256]{4,3,2,1,0:T(8,128)} %bitcast.4, f32[5,4,4,32,256]{4,3,2,1,0:T(8,128)} %bitcast.5, s32[4,256]{1,0:T(4,128)} %nb_in.1), custom_call_target="tpu_custom_call" | custom-call | tf_op jit(solution)/shard_map/exchange/pallas_call | solution.py:374
  12.0 0.0 copy-done
  12.0 3.5 %surface.1 = (f32[5,4,4,32,256]{4,3,2,1,0:T(8,128)}, f32[5,4,4,32,256]{4,3,2,1,0:T(8,128)}) custom-call(f32[5,4,4,32,256]{4,3,2,1,0:T(8,128)S(1)} %get-tuple-element.8.cv, f32[5,4,4,32,256]{4,3,2,1,0:T(8,128)S(1)} %get-tuple-element.9.acc, f32[4,5,4,32,256]{4,3,2,1,0:T(8,128)S(1)} %get-tuple-element.10.ghost, f32[2,80,256]{2,1,0:T(8,128)S(1)} %get-tuple-element.11.vert, ...), custom_call_target="tpu_custom_call" | custom-call | tf_op jit(solution)/shard_map/surface/pallas_call | solution.py:407
Async XLA Ops:
  0.6 11.4 %copy-start = (s32[4,256]{1,0:T(4,128)S(1)}, s32[4,256]{1,0:T(4,128)}, u32[]{:S(2)}) copy-start(s32[4,256]{1,0:T(4,128)} %kinds.1) | copy-start | bytes 12292

commit v5 on v4

--- a/solution.py
+++ b/solution.py
@@ -95,8 +95,8 @@
 
 
 def exchange_kernel(
-    cons, reg, nb_in, cv, acc, ghost, vert,
-    nb, regv, prim, halves, picks, stage, packed, arrived, sendv, recvv,
+    cons, reg, nb_in, cv, acc, ghost, vert, prim,
+    nb, regv, picks, stage, packed, arrived, sendv, recvv,
     load_sem, send_sem, recv_sem, vsend_sem, vrecv_sem,
 ):
     foot, layer = lax.axis_index("foot"), lax.axis_index("layer")
@@ -131,7 +131,6 @@
     for copy in loads:
         copy.start()
     reg_load = pltpu.make_async_copy(reg, regv, load_sem.at[5])
-    reg_load.start()
 
     slot = lax.bitwise_and(lax.broadcasted_iota(jnp.int32, (128, 256), 0), SLOTS - 1)
     lane_z = lax.broadcasted_iota(jnp.int32, (80, 128), 1) // SLOTS
@@ -147,6 +146,7 @@
 
     for copy in loads:
         copy.wait()
+    reg_load.start()
 
     for way in (0, 1):
         for h in (0, 1):
@@ -155,8 +155,6 @@
             sendv[way, :, lanes] = stage[2 * way + h, pl.ds(7 * way, 80, stride=8), :]
     for side in range(4):
         hi, lo = split(trace_of(cv, side))
-        halves[side, :, 0:256] = hi
-        halves[side, :, 256:512] = lo
         send = jnp.where(rank[side:side + 1] == slot, 1.0, 0.0).astype(BF16)
         stage[side] = dot_nt(hi, send) + dot_nt(lo, send)
         packed[side ^ 1] = gather_slots(stage, side, lane_z)
@@ -185,13 +183,14 @@
         flux = [[], [], [], [], []]
         for k in range(4):
             rho, mx, my, mz, energy = (q[v][k] for v in range(5))
-            r = inverse(rho)
-            pressure = 0.4 * energy - 0.2 * ((mx * mx + my * my + mz * mz) * r)
+            r, pressure, sound = primitive([q[v][k] for v in range(5)])
             vz = mz * r
             rows_k = pl.ds(8 * k, 8)
             prim[0, i, j, rows_k, :] = mx * r
             prim[1, i, j, rows_k, :] = my * r
-            prim[2, i, j, rows_k, :] = pressure
+            prim[2, i, j, rows_k, :] = vz
+            prim[3, i, j, rows_k, :] = pressure
+            prim[4, i, j, rows_k, :] = sound
             flux[0].append(mz)
             flux[1].append(mx * vz)
             flux[2].append(my * vz)
@@ -217,7 +216,7 @@
         flux = [[], [], [], [], []]
         for node in range(4):
             vd = prim[(direction,) + at(node)]
-            pressure = prim[(2,) + at(node)]
+            pressure = prim[(3,) + at(node)]
             m = [cv[(1 + c,) + at(node)] for c in range(3)]
             flux[0].append(m[direction])
             for c in range(3):
@@ -250,6 +249,12 @@
     lane_z3 = lax.broadcasted_iota(jnp.int32, (80, 8, 128), 2) // SLOTS
     sub_z3 = lax.broadcasted_iota(jnp.int32, (80, 8, 128), 1)
     for side in range(4):
+        select = jnp.where(here[side:side + 1] == rows, 1.0, 0.0).astype(BF16)
+        hi, lo = split(trace_of(cv, side ^ 1))
+        got = dot(hi, select) + dot(lo, select)
+        ghost[side] = got.reshape(5, 4, 32, 256)
+
+    for side in range(4):
         _, there, comes = sends[side]
 
         @pl.when(there)
@@ -266,10 +271,9 @@
 
         spread = jnp.where(lane_z3 == sub_z3, arrived[side][:, None, :], 0.0).reshape(640, 128)
         far_hi, far_lo = split(spread)
-        select = jnp.where(here[side:side + 1] == rows, 1.0, 0.0).astype(BF16)
-        left_side = jnp.concatenate([halves[side ^ 1], far_hi, far_lo], axis=1)
-        right_side = jnp.concatenate([select, select, picks[side], picks[side]], axis=0)
-        ghost[side] = dot(left_side, right_side).reshape(5, 4, 32, 256)
+        both = jnp.concatenate([far_hi, far_lo], axis=1)
+        twice = jnp.concatenate([picks[side], picks[side]], axis=0)
+        ghost[side] = ghost[side] + dot(both, twice).reshape(5, 4, 32, 256)
 
     for way in (0, 1):
         _, there, comes = sends[4 + way]
@@ -293,17 +297,17 @@
         vert[1, part, :] = jnp.where(above, recvv[0, part, :], jnp.full_like(own, FREE_STREAM[v]))
 
 
-def surface_kernel(cv, acc, ghost, vert, kinds, adv, new, adv_v, new_v, out_sem):
+def surface_kernel(cv, acc, ghost, vert, prim, kinds, adv, new, adv_v, new_v, out_sem):
     sub = lax.broadcasted_iota(jnp.int32, (8, 128), 0)
     outs = []
     for i in range(4):
 
-        def half(h, carry):
+        def half(js, h, carry):
             lanes = pl.ds(pl.multiple_of(h * 128, 128), 128)
             kind = [jnp.broadcast_to(kinds[s:s + 1, lanes], (8, 128)) for s in range(4)]
             open_face = [kind[s] == 0 for s in range(4)]
             wall = [kind[s] == 1 for s in range(4)]
-            for j in range(4):
+            for j in js:
                 for k in range(4):
                     rows_k = pl.ds(8 * k, 8)
                     q = [cv[v, i, j, rows_k, lanes] for v in range(5)]
@@ -316,7 +320,7 @@
                     if k in (0, 3):
                         faces.append((2, 4 if k == 0 else 5, (i, j)))
                     if faces:
-                        r_in, p_in, c_in = primitive(q)
+                        p_in, c_in = (prim[v, i, j, rows_k, lanes] for v in (3, 4))
                     for d, side, (a, b) in faces:
                         if side < 4:
                             outer = []
@@ -341,7 +345,7 @@
                                     outer.append(jnp.where(sub == 7, edge, near))
                         sign = -1.0 if side % 2 == 0 else 1.0
                         r_out, p_out, c_out = primitive(outer)
-                        v_in, v_out = q[1 + d] * r_in, outer[1 + d] * r_out
+                        v_in, v_out = prim[d, i, j, rows_k, lanes], outer[1 + d] * r_out
                         lam = LIFT * jnp.maximum(jnp.abs(v_in) + c_in, jnp.abs(v_out) + c_out)
                         s_in, s_out = (sign * LIFT) * v_in, (sign * LIFT) * v_out
                         w_in, w_out = lam - s_in, lam - s_out
@@ -354,11 +358,14 @@
                         adv_v[v, i, j, rows_k, lanes] = q[v] + SECTION_WEIGHT * total[v]
             return carry
 
-        lax.fori_loop(0, 2, half, 0)
-        for n, (src, dst) in enumerate(((adv_v, adv), (new_v, new))):
-            copy = pltpu.make_async_copy(src.at[:, i], dst.at[:, i], out_sem.at[n, i])
-            copy.start()
-            outs.append(copy)
+        for part in range(2):
+            js = (2 * part, 2 * part + 1)
+            lax.fori_loop(0, 2, functools.partial(half, js), 0)
+            for n, (src, dst) in enumerate(((adv_v, adv), (new_v, new))):
+                js_here = pl.ds(2 * part, 2)
+                copy = pltpu.make_async_copy(src.at[:, i, js_here], dst.at[:, i, js_here], out_sem.at[n, 2 * i + part])
+                copy.start()
+                outs.append(copy)
     for copy in outs:
         copy.wait()
 
@@ -379,14 +386,13 @@
             pltpu.VMEM(SHAPE, F32),
             pltpu.VMEM((4, 5, 4, 32, 256), F32),
             pltpu.VMEM((2, 80, 256), F32),
+            pltpu.VMEM(SHAPE, F32),
         ),
         in_specs=[pl.BlockSpec(memory_space=pltpu.HBM)] * 3,
-        out_specs=tuple([pl.BlockSpec(memory_space=pltpu.VMEM)] * 4),
+        out_specs=tuple([pl.BlockSpec(memory_space=pltpu.VMEM)] * 5),
         scratch_shapes=[
             pltpu.VMEM((4, 256), jnp.int32),
             pltpu.VMEM(SHAPE, F32),
-            pltpu.VMEM((3, 4, 4, 32, 256), F32),
-            pltpu.VMEM((4, 640, 512), BF16),
             pltpu.VMEM((4, 128, 256), BF16),
             pltpu.VMEM((4, 640, 128), F32),
             pltpu.VMEM((4, 80, 128), F32),
@@ -408,12 +414,12 @@
         surface_kernel,
         name="surface",
         out_shape=(jax.ShapeDtypeStruct(SHAPE, F32), jax.ShapeDtypeStruct(SHAPE, F32)),
-        in_specs=[pl.BlockSpec(memory_space=pltpu.VMEM)] * 5,
+        in_specs=[pl.BlockSpec(memory_space=pltpu.VMEM)] * 6,
         out_specs=(pl.BlockSpec(memory_space=pltpu.HBM), pl.BlockSpec(memory_space=pltpu.HBM)),
         scratch_shapes=[
             pltpu.VMEM(SHAPE, F32),
             pltpu.VMEM(SHAPE, F32),
-            pltpu.SemaphoreType.DMA((2, 4)),
+            pltpu.SemaphoreType.DMA((2, 8)),
         ],
         compiler_params=pltpu.CompilerParams(vmem_limit_bytes=32 * 1024 * 1024),
     )(*handed, side_type)

time: 15.6 us -> 14.3 us (0.917)
  Pallas kernels: 14.9 us -> 13.6 us
    pallas_call x1, Pallas kernels: 11.3 us -> 10.3 us  [per_device(): pl.pallas_call(exchange_kernel, name='exchange', out_shape=(pltpu.VMEM(SH...]
    pallas_call x1, Pallas kernels: 3.51 us -> 3.25 us  [per_device(): pl.pallas_call(surface_kernel, name='surface', out_shape=(jax.ShapeDtypeS...]
where the time goes in v5:
time: 14.3 us; the launch traced here: 14.2 us
  Pallas kernels  13.6 us (95%)
  between operations  0.65 us (5%)
    pallas_call x1, Pallas kernels, per_device(): pl.pallas_call(exchange_kernel, name='exchange', out_shape=(pltpu.VMEM(SH...  10.3 us
    pallas_call x1, Pallas kernels, per_device(): pl.pallas_call(surface_kernel, name='surface', out_shape=(jax.ShapeDtypeS...  3.25 us

profile of v5, /device:TPU:102, one launch (start us, length us, event | category | flops | bytes accessed | tf_op | source)
XLA Modules:
  0.0 14.2 jit_solution(1596451063368646930)
XLA Ops:
  0.6 0.0 copy-start
  0.6 10.3 %exchange.1 = (f32[5,4,4,32,256]{4,3,2,1,0:T(8,128)S(1)}, f32[5,4,4,32,256]{4,3,2,1,0:T(8,128)S(1)}, f32[4,5,4,32,256]{4,3,2,1,0:T(8,128)S(1)}, f32[2,80,256]{2,1,0:T(8,128)S(1)}, f32[5,4,4,32,256]{4,3,2,1,0:T(8,128)S(1)}) custom-call(f32[5,4,4,32,256]{4,3,2,1,0:T(8,128)} %bitcast.4, f32[5,4,4,32,256]{4,3,2,1,0:T(8,128)} %bitcast.5, s32[4,256]{1,0:T(4,128)} %nb_in.1), custom_call_target="tpu_custom_call" | custom-call | tf_op jit(solution)/shard_map/exchange/pallas_call | solution.py:381
  11.0 0.0 copy-done
  11.0 3.2 %surface.1 = (f32[5,4,4,32,256]{4,3,2,1,0:T(8,128)}, f32[5,4,4,32,256]{4,3,2,1,0:T(8,128)}) custom-call(f32[5,4,4,32,256]{4,3,2,1,0:T(8,128)S(1)} %get-tuple-element.9.cv, f32[5,4,4,32,256]{4,3,2,1,0:T(8,128)S(1)} %get-tuple-element.10.acc, f32[4,5,4,32,256]{4,3,2,1,0:T(8,128)S(1)} %get-tuple-element.11.ghost, f32[2,80,256]{2,1,0:T(8,128)S(1)} %get-tuple-element.12.vert, ...), custom_call_target="tpu_custom_call" | custom-call | tf_op jit(solution)/shard_map/surface/pallas_call | solution.py:413
Async XLA Ops:
  0.6 10.3 %copy-start = (s32[4,256]{1,0:T(4,128)S(1)}, s32[4,256]{1,0:T(4,128)}, u32[]{:S(2)}) copy-start(s32[4,256]{1,0:T(4,128)} %kinds.1) | copy-start | bytes 12292

commit v6 on v5

--- a/solution.py
+++ b/solution.py
@@ -96,7 +96,7 @@
 
 def exchange_kernel(
     cons, reg, nb_in, cv, acc, ghost, vert, prim,
-    nb, regv, picks, stage, packed, arrived, sendv, recvv,
+    nb, regv, picks, send_picks, selects, stage, packed, arrived, sendv, recvv,
     load_sem, send_sem, recv_sem, vsend_sem, vrecv_sem,
 ):
     foot, layer = lax.axis_index("foot"), lax.axis_index("layer")
@@ -144,6 +144,14 @@
     mask8 = jnp.concatenate([mask, jnp.zeros_like(mask)], axis=0).astype(BF16)
     rank = jnp.where(away, dot(mask8, before)[0:4], -1.0).astype(jnp.int32)
 
+    names = jnp.where(away, lax.bitwise_and(nb[...], 255), 1000).astype(F32)
+    names_down = jnp.transpose(jnp.concatenate([names, names], axis=0))
+    for side in range(4):
+        less = jnp.where(names_down[:, side:side + 1] < names[side:side + 1], 1.0, 0.0)
+        order = jnp.sum(less, axis=0, keepdims=True)
+        order = jnp.where(away[side:side + 1], order, -1.0).astype(jnp.int32)
+        picks[side] = jnp.where(order == slot, 1.0, 0.0).astype(BF16)
+
     for copy in loads:
         copy.wait()
     reg_load.start()
@@ -153,11 +161,6 @@
             lanes = pl.ds(h * 128, 128)
             stage[2 * way + h] = cv[:, :, :, pl.ds(24 * way, 8), lanes].reshape(640, 128)
             sendv[way, :, lanes] = stage[2 * way + h, pl.ds(7 * way, 80, stride=8), :]
-    for side in range(4):
-        hi, lo = split(trace_of(cv, side))
-        send = jnp.where(rank[side:side + 1] == slot, 1.0, 0.0).astype(BF16)
-        stage[side] = dot_nt(hi, send) + dot_nt(lo, send)
-        packed[side ^ 1] = gather_slots(stage, side, lane_z)
 
     pl.semaphore_wait(barrier, partners)
     copies = []
@@ -171,11 +174,22 @@
             src_ref=sendv.at[way], dst_ref=recvv.at[way], send_sem=vsend_sem.at[way],
             recv_sem=vrecv_sem.at[way], device_id=sends[4 + way][0], device_id_type=MESH,
         ))
-    for copy, (_, there, _) in zip(copies, sends):
-
-        @pl.when(there)
-        def _():
-            copy.start()
+    def launch(which):
+        for copy, (_, there, _) in list(zip(copies, sends))[which]:
+
+            @pl.when(there)
+            def _():
+                copy.start()
+
+    launch(slice(4, 6))
+
+    for side in range(4):
+        hi, lo = split(trace_of(cv, side))
+        send = jnp.where(rank[side:side + 1] == slot, 1.0, 0.0).astype(BF16)
+        stage[side] = dot_nt(hi, send) + dot_nt(lo, send)
+        packed[side ^ 1] = gather_slots(stage, side, lane_z)
+
+    launch(slice(0, 4))
 
     def z_lines(line, carry):
         i, j = line // 4, line % 4
@@ -203,7 +217,7 @@
                 acc[v, i, j, rows_k, :] = out[k]
         return carry
 
-    lax.fori_loop(0, 16, z_lines, 0)
+    lax.fori_loop(0, 16, z_lines, 0, unroll=4)
 
 
     def lines(direction, line, carry):
@@ -234,26 +248,19 @@
                 acc[(v,) + at(node)] = total
         return carry
 
-    lax.fori_loop(0, 16, functools.partial(lines, 0), 0)
+    lax.fori_loop(0, 16, functools.partial(lines, 0), 0, unroll=4)
     reg_load.wait()
-    lax.fori_loop(0, 16, functools.partial(lines, 1), 0)
-
-    names = jnp.where(away, lax.bitwise_and(nb[...], 255), 1000).astype(F32)
-    names_down = jnp.transpose(jnp.concatenate([names, names], axis=0))
+    lax.fori_loop(0, 16, functools.partial(lines, 1), 0, unroll=4)
+
     for side in range(4):
-        less = jnp.where(names_down[:, side:side + 1] < names[side:side + 1], 1.0, 0.0)
-        order = jnp.sum(less, axis=0, keepdims=True)
-        order = jnp.where(away[side:side + 1], order, -1.0).astype(jnp.int32)
-        picks[side] = jnp.where(order == slot, 1.0, 0.0).astype(BF16)
+        hi, lo = split(trace_of(cv, side))
+        select = jnp.where(here[(side ^ 1):(side ^ 1) + 1] == rows, 1.0, 0.0).astype(BF16)
+        got = dot(jnp.concatenate([hi, lo], axis=0), select)
+        got = got[:640] + got[640:]
+        ghost[side ^ 1] = got.reshape(5, 4, 32, 256)
 
     lane_z3 = lax.broadcasted_iota(jnp.int32, (80, 8, 128), 2) // SLOTS
     sub_z3 = lax.broadcasted_iota(jnp.int32, (80, 8, 128), 1)
-    for side in range(4):
-        select = jnp.where(here[side:side + 1] == rows, 1.0, 0.0).astype(BF16)
-        hi, lo = split(trace_of(cv, side ^ 1))
-        got = dot(hi, select) + dot(lo, select)
-        ghost[side] = got.reshape(5, 4, 32, 256)
-
     for side in range(4):
         _, there, comes = sends[side]
 
@@ -394,6 +401,8 @@
             pltpu.VMEM((4, 256), jnp.int32),
             pltpu.VMEM(SHAPE, F32),
             pltpu.VMEM((4, 128, 256), BF16),
+            pltpu.VMEM((4, 128, 256), BF16),
+            pltpu.VMEM((4, 256, 256), BF16),
             pltpu.VMEM((4, 640, 128), F32),
             pltpu.VMEM((4, 80, 128), F32),
             pltpu.VMEM((4, 80, 128), F32),

time: 14.3 us -> 15.3 us (1.070)
  Pallas kernels: 13.6 us -> 14.5 us
    pallas_call x1, Pallas kernels: 10.3 us -> 11.3 us  [per_device(): pl.pallas_call(exchange_kernel, name='exchange', out_shape=(pltpu.VMEM(SH...]
where the time goes in v6:
time: 15.3 us; the launch traced here: 15.2 us
  Pallas kernels  14.5 us (95%)
  between operations  0.65 us (4%)
    pallas_call x1, Pallas kernels, per_device(): pl.pallas_call(exchange_kernel, name='exchange', out_shape=(pltpu.VMEM(SH...  11.3 us
    pallas_call x1, Pallas kernels, per_device(): pl.pallas_call(surface_kernel, name='surface', out_shape=(jax.ShapeDtypeS...  3.25 us

profile of v6, /device:TPU:102, one launch (start us, length us, event | category | flops | bytes accessed | tf_op | source)
XLA Modules:
  0.0 15.2 jit_solution(980597898924609593)
XLA Ops:
  0.6 0.0 copy-start
  0.6 11.3 %exchange.1 = (f32[5,4,4,32,256]{4,3,2,1,0:T(8,128)S(1)}, f32[5,4,4,32,256]{4,3,2,1,0:T(8,128)S(1)}, f32[4,5,4,32,256]{4,3,2,1,0:T(8,128)S(1)}, f32[2,80,256]{2,1,0:T(8,128)S(1)}, f32[5,4,4,32,256]{4,3,2,1,0:T(8,128)S(1)}) custom-call(f32[5,4,4,32,256]{4,3,2,1,0:T(8,128)} %bitcast.4, f32[5,4,4,32,256]{4,3,2,1,0:T(8,128)} %bitcast.5, s32[4,256]{1,0:T(4,128)} %nb_in.1), custom_call_target="tpu_custom_call" | custom-call | tf_op jit(solution)/shard_map/exchange/pallas_call | solution.py:388
  11.9 0.0 copy-done
  11.9 3.2 %surface.1 = (f32[5,4,4,32,256]{4,3,2,1,0:T(8,128)}, f32[5,4,4,32,256]{4,3,2,1,0:T(8,128)}) custom-call(f32[5,4,4,32,256]{4,3,2,1,0:T(8,128)S(1)} %get-tuple-element.9.cv, f32[5,4,4,32,256]{4,3,2,1,0:T(8,128)S(1)} %get-tuple-element.10.acc, f32[4,5,4,32,256]{4,3,2,1,0:T(8,128)S(1)} %get-tuple-element.11.ghost, f32[2,80,256]{2,1,0:T(8,128)S(1)} %get-tuple-element.12.vert, ...), custom_call_target="tpu_custom_call" | custom-call | tf_op jit(solution)/shard_map/surface/pallas_call | solution.py:422
Async XLA Ops:
  0.6 11.3 %copy-start = (s32[4,256]{1,0:T(4,128)S(1)}, s32[4,256]{1,0:T(4,128)}, u32[]{:S(2)}) copy-start(s32[4,256]{1,0:T(4,128)} %kinds.1) | copy-start | bytes 12292

commit v7 on v6

--- a/solution.py
+++ b/solution.py
@@ -127,7 +127,10 @@
 
     nb_load = pltpu.make_async_copy(nb_in, nb, load_sem.at[6])
     nb_load.start()
-    loads = [pltpu.make_async_copy(cons.at[v], cv.at[v], load_sem.at[v]) for v in range(5)]
+    loads = [
+        pltpu.make_async_copy(cons.at[:, :, :, part], cv.at[:, :, :, part], load_sem.at[n])
+        for n, part in enumerate((pl.ds(0, 8), pl.ds(24, 8), pl.ds(8, 16)))
+    ]
     for copy in loads:
         copy.start()
     reg_load = pltpu.make_async_copy(reg, regv, load_sem.at[5])
@@ -144,19 +147,8 @@
     mask8 = jnp.concatenate([mask, jnp.zeros_like(mask)], axis=0).astype(BF16)
     rank = jnp.where(away, dot(mask8, before)[0:4], -1.0).astype(jnp.int32)
 
-    names = jnp.where(away, lax.bitwise_and(nb[...], 255), 1000).astype(F32)
-    names_down = jnp.transpose(jnp.concatenate([names, names], axis=0))
-    for side in range(4):
-        less = jnp.where(names_down[:, side:side + 1] < names[side:side + 1], 1.0, 0.0)
-        order = jnp.sum(less, axis=0, keepdims=True)
-        order = jnp.where(away[side:side + 1], order, -1.0).astype(jnp.int32)
-        picks[side] = jnp.where(order == slot, 1.0, 0.0).astype(BF16)
-
-    for copy in loads:
-        copy.wait()
-    reg_load.start()
-
     for way in (0, 1):
+        loads[way].wait()
         for h in (0, 1):
             lanes = pl.ds(h * 128, 128)
             stage[2 * way + h] = cv[:, :, :, pl.ds(24 * way, 8), lanes].reshape(640, 128)
@@ -182,6 +174,17 @@
                 copy.start()
 
     launch(slice(4, 6))
+
+    names = jnp.where(away, lax.bitwise_and(nb[...], 255), 1000).astype(F32)
+    names_down = jnp.transpose(jnp.concatenate([names, names], axis=0))
+    for side in range(4):
+        less = jnp.where(names_down[:, side:side + 1] < names[side:side + 1], 1.0, 0.0)
+        order = jnp.sum(less, axis=0, keepdims=True)
+        order = jnp.where(away[side:side + 1], order, -1.0).astype(jnp.int32)
+        picks[side] = jnp.where(order == slot, 1.0, 0.0).astype(BF16)
+
+    loads[2].wait()
+    reg_load.start()
 
     for side in range(4):
         hi, lo = split(trace_of(cv, side))

time: 15.3 us -> 15.7 us (1.026)
  Pallas kernels: 14.5 us -> 14.9 us
    pallas_call x1, Pallas kernels: 11.3 us -> 11.7 us  [per_device(): pl.pallas_call(exchange_kernel, name='exchange', out_shape=(pltpu.VMEM(SH...]
where the time goes in v7:
time: 15.7 us; the launch traced here: 15.6 us
  Pallas kernels  14.9 us (95%)
  between operations  0.65 us (4%)
    pallas_call x1, Pallas kernels, per_device(): pl.pallas_call(exchange_kernel, name='exchange', out_shape=(pltpu.VMEM(SH...  11.7 us
    pallas_call x1, Pallas kernels, per_device(): pl.pallas_call(surface_kernel, name='surface', out_shape=(jax.ShapeDtypeS...  3.25 us

profile of v7, /device:TPU:102, one launch (start us, length us, event | category | flops | bytes accessed | tf_op | source)
XLA Modules:
  0.0 15.6 jit_solution(9291897162670760156)
XLA Ops:
  0.6 0.0 copy-start
  0.6 11.7 %exchange.1 = (f32[5,4,4,32,256]{4,3,2,1,0:T(8,128)S(1)}, f32[5,4,4,32,256]{4,3,2,1,0:T(8,128)S(1)}, f32[4,5,4,32,256]{4,3,2,1,0:T(8,128)S(1)}, f32[2,80,256]{2,1,0:T(8,128)S(1)}, f32[5,4,4,32,256]{4,3,2,1,0:T(8,128)S(1)}) custom-call(f32[5,4,4,32,256]{4,3,2,1,0:T(8,128)} %bitcast.4, f32[5,4,4,32,256]{4,3,2,1,0:T(8,128)} %bitcast.5, s32[4,256]{1,0:T(4,128)} %nb_in.1), custom_call_target="tpu_custom_call" | custom-call | tf_op jit(solution)/shard_map/exchange/pallas_call | solution.py:391
  12.3 0.0 copy-done
  12.3 3.2 %surface.1 = (f32[5,4,4,32,256]{4,3,2,1,0:T(8,128)}, f32[5,4,4,32,256]{4,3,2,1,0:T(8,128)}) custom-call(f32[5,4,4,32,256]{4,3,2,1,0:T(8,128)S(1)} %get-tuple-element.9.cv, f32[5,4,4,32,256]{4,3,2,1,0:T(8,128)S(1)} %get-tuple-element.10.acc, f32[4,5,4,32,256]{4,3,2,1,0:T(8,128)S(1)} %get-tuple-element.11.ghost, f32[2,80,256]{2,1,0:T(8,128)S(1)} %get-tuple-element.12.vert, ...), custom_call_target="tpu_custom_call" | custom-call | tf_op jit(solution)/shard_map/surface/pallas_call | solution.py:425
Async XLA Ops:
  0.6 11.7 %copy-start = (s32[4,256]{1,0:T(4,128)S(1)}, s32[4,256]{1,0:T(4,128)}, u32[]{:S(2)}) copy-start(s32[4,256]{1,0:T(4,128)} %kinds.1) | copy-start | bytes 12292

commit v8 on v7

--- a/solution.py
+++ b/solution.py
@@ -154,7 +154,6 @@
             stage[2 * way + h] = cv[:, :, :, pl.ds(24 * way, 8), lanes].reshape(640, 128)
             sendv[way, :, lanes] = stage[2 * way + h, pl.ds(7 * way, 80, stride=8), :]
 
-    pl.semaphore_wait(barrier, partners)
     copies = []
     for side in range(4):
         copies.append(pltpu.make_async_remote_copy(
@@ -173,7 +172,6 @@
             def _():
                 copy.start()
 
-    launch(slice(4, 6))
 
     names = jnp.where(away, lax.bitwise_and(nb[...], 255), 1000).astype(F32)
     names_down = jnp.transpose(jnp.concatenate([names, names], axis=0))
@@ -186,12 +184,20 @@
     loads[2].wait()
     reg_load.start()
 
+    def open_vertical():
+        pl.semaphore_wait(barrier, partners)
+        launch(slice(4, 6))
+
+    first = layer == layers // 2 - 1
+    pl.when(first)(open_vertical)
+
     for side in range(4):
         hi, lo = split(trace_of(cv, side))
         send = jnp.where(rank[side:side + 1] == slot, 1.0, 0.0).astype(BF16)
         stage[side] = dot_nt(hi, send) + dot_nt(lo, send)
         packed[side ^ 1] = gather_slots(stage, side, lane_z)
 
+    pl.when(jnp.logical_not(first))(open_vertical)
     launch(slice(0, 4))
 
     def z_lines(line, carry):

time: 15.7 us -> 14.3 us (0.911)
  Pallas kernels: 14.9 us -> 13.6 us
    pallas_call x1, Pallas kernels: 11.7 us -> 10.3 us  [per_device(): pl.pallas_call(exchange_kernel, name='exchange', out_shape=(pltpu.VMEM(SH...]
where the time goes in v8:
time: 14.3 us; the launch traced here: 14.2 us
  Pallas kernels  13.6 us (95%)
  between operations  0.65 us (5%)
    pallas_call x1, Pallas kernels, per_device(): pl.pallas_call(exchange_kernel, name='exchange', out_shape=(pltpu.VMEM(SH...  10.3 us
    pallas_call x1, Pallas kernels, per_device(): pl.pallas_call(surface_kernel, name='surface', out_shape=(jax.ShapeDtypeS...  3.25 us

profile of v8, /device:TPU:102, one launch (start us, length us, event | category | flops | bytes accessed | tf_op | source)
XLA Modules:
  0.0 14.2 jit_solution(13834525443125936186)
XLA Ops:
  0.6 0.0 copy-start
  0.6 10.3 %exchange.1 = (f32[5,4,4,32,256]{4,3,2,1,0:T(8,128)S(1)}, f32[5,4,4,32,256]{4,3,2,1,0:T(8,128)S(1)}, f32[4,5,4,32,256]{4,3,2,1,0:T(8,128)S(1)}, f32[2,80,256]{2,1,0:T(8,128)S(1)}, f32[5,4,4,32,256]{4,3,2,1,0:T(8,128)S(1)}) custom-call(f32[5,4,4,32,256]{4,3,2,1,0:T(8,128)} %bitcast.4, f32[5,4,4,32,256]{4,3,2,1,0:T(8,128)} %bitcast.5, s32[4,256]{1,0:T(4,128)} %nb_in.1), custom_call_target="tpu_custom_call" | custom-call | tf_op jit(solution)/shard_map/exchange/pallas_call | solution.py:397
  11.0 0.0 copy-done
  11.0 3.2 %surface.1 = (f32[5,4,4,32,256]{4,3,2,1,0:T(8,128)}, f32[5,4,4,32,256]{4,3,2,1,0:T(8,128)}) custom-call(f32[5,4,4,32,256]{4,3,2,1,0:T(8,128)S(1)} %get-tuple-element.9.cv, f32[5,4,4,32,256]{4,3,2,1,0:T(8,128)S(1)} %get-tuple-element.10.acc, f32[4,5,4,32,256]{4,3,2,1,0:T(8,128)S(1)} %get-tuple-element.11.ghost, f32[2,80,256]{2,1,0:T(8,128)S(1)} %get-tuple-element.12.vert, ...), custom_call_target="tpu_custom_call" | custom-call | tf_op jit(solution)/shard_map/surface/pallas_call | solution.py:431
Async XLA Ops:
  0.6 10.3 %copy-start = (s32[4,256]{1,0:T(4,128)S(1)}, s32[4,256]{1,0:T(4,128)}, u32[]{:S(2)}) copy-start(s32[4,256]{1,0:T(4,128)} %kinds.1) | copy-start | bytes 12292

commit v9 on v8

--- a/solution.py
+++ b/solution.py
@@ -95,8 +95,8 @@
 
 
 def exchange_kernel(
-    cons, reg, nb_in, cv, acc, ghost, vert, prim,
-    nb, regv, picks, send_picks, selects, stage, packed, arrived, sendv, recvv,
+    cons, reg, nb_in, kinds_in, cv, acc, ghost, vert, prim,
+    nb, kinds, regv, picks, send_picks, selects, stage, packed, arrived, sendv, recvv,
     load_sem, send_sem, recv_sem, vsend_sem, vrecv_sem,
 ):
     foot, layer = lax.axis_index("foot"), lax.axis_index("layer")
@@ -127,6 +127,8 @@
 
     nb_load = pltpu.make_async_copy(nb_in, nb, load_sem.at[6])
     nb_load.start()
+    kinds_load = pltpu.make_async_copy(kinds_in, kinds, load_sem.at[7])
+    kinds_load.start()
     loads = [
         pltpu.make_async_copy(cons.at[:, :, :, part], cv.at[:, :, :, part], load_sem.at[n])
         for n, part in enumerate((pl.ds(0, 8), pl.ds(24, 8), pl.ds(8, 16)))
@@ -181,6 +183,7 @@
         order = jnp.where(away[side:side + 1], order, -1.0).astype(jnp.int32)
         picks[side] = jnp.where(order == slot, 1.0, 0.0).astype(BF16)
 
+    kinds_load.wait()
     loads[2].wait()
     reg_load.start()
 
@@ -289,7 +292,15 @@
         far_hi, far_lo = split(spread)
         both = jnp.concatenate([far_hi, far_lo], axis=1)
         twice = jnp.concatenate([picks[side], picks[side]], axis=0)
-        ghost[side] = ghost[side] + dot(both, twice).reshape(5, 4, 32, 256)
+        got = ghost[side].reshape(640, 256) + dot(both, twice)
+        own = trace_of(cv, side)
+        kind = jnp.broadcast_to(kinds[side:side + 1], (128, 256))
+        flip = jnp.where(kind == 1, -1.0, 1.0)
+        for v in range(5):
+            part = slice(128 * v, 128 * v + 128)
+            inner = own[part] * flip if v == 1 + side // 2 else own[part]
+            outer = jnp.where(kind == 0, got[part], jnp.where(kind == 2, FREE_STREAM[v], inner))
+            ghost[side, v] = outer.reshape(4, 32, 256)
 
     for way in (0, 1):
         _, there, comes = sends[4 + way]
@@ -313,16 +324,13 @@
         vert[1, part, :] = jnp.where(above, recvv[0, part, :], jnp.full_like(own, FREE_STREAM[v]))
 
 
-def surface_kernel(cv, acc, ghost, vert, prim, kinds, adv, new, adv_v, new_v, out_sem):
+def surface_kernel(cv, acc, ghost, vert, prim, adv, new, adv_v, new_v, out_sem):
     sub = lax.broadcasted_iota(jnp.int32, (8, 128), 0)
     outs = []
     for i in range(4):
 
         def half(js, h, carry):
             lanes = pl.ds(pl.multiple_of(h * 128, 128), 128)
-            kind = [jnp.broadcast_to(kinds[s:s + 1, lanes], (8, 128)) for s in range(4)]
-            open_face = [kind[s] == 0 for s in range(4)]
-            wall = [kind[s] == 1 for s in range(4)]
             for j in js:
                 for k in range(4):
                     rows_k = pl.ds(8 * k, 8)
@@ -339,12 +347,7 @@
                         p_in, c_in = (prim[v, i, j, rows_k, lanes] for v in (3, 4))
                     for d, side, (a, b) in faces:
                         if side < 4:
-                            outer = []
-                            for v in range(5):
-                                inner = -q[v] if v == 1 + d else q[v]
-                                other = jnp.where(wall[side], inner, FREE_STREAM[v])
-                                got = ghost[side, v, a, pl.ds(8 * b, 8), lanes]
-                                outer.append(jnp.where(open_face[side], got, other))
+                            outer = [ghost[side, v, a, pl.ds(8 * b, 8), lanes] for v in range(5)]
                         else:
                             outer = []
                             for v in range(5):
@@ -392,7 +395,7 @@
 def per_device(conserved, register, neighbour, side_type):
     inputs = [
         pltpu.with_memory_space_constraint(x, pltpu.HBM)
-        for x in (conserved.reshape(SHAPE), register.reshape(SHAPE), neighbour)
+        for x in (conserved.reshape(SHAPE), register.reshape(SHAPE), neighbour, side_type)
     ]
     handed = pl.pallas_call(
         exchange_kernel,
@@ -404,9 +407,10 @@
             pltpu.VMEM((2, 80, 256), F32),
             pltpu.VMEM(SHAPE, F32),
         ),
-        in_specs=[pl.BlockSpec(memory_space=pltpu.HBM)] * 3,
+        in_specs=[pl.BlockSpec(memory_space=pltpu.HBM)] * 4,
         out_specs=tuple([pl.BlockSpec(memory_space=pltpu.VMEM)] * 5),
         scratch_shapes=[
+            pltpu.VMEM((4, 256), jnp.int32),
             pltpu.VMEM((4, 256), jnp.int32),
             pltpu.VMEM(SHAPE, F32),
             pltpu.VMEM((4, 128, 256), BF16),
@@ -417,7 +421,7 @@
             pltpu.VMEM((4, 80, 128), F32),
             pltpu.VMEM((2, 80, 256), F32),
             pltpu.VMEM((2, 80, 256), F32),
-            pltpu.SemaphoreType.DMA((7,)),
+            pltpu.SemaphoreType.DMA((8,)),
             pltpu.SemaphoreType.DMA((4,)),
             pltpu.SemaphoreType.DMA((4,)),
             pltpu.SemaphoreType.DMA((2,)),
@@ -432,7 +436,7 @@
         surface_kernel,
         name="surface",
         out_shape=(jax.ShapeDtypeStruct(SHAPE, F32), jax.ShapeDtypeStruct(SHAPE, F32)),
-        in_specs=[pl.BlockSpec(memory_space=pltpu.VMEM)] * 6,
+        in_specs=[pl.BlockSpec(memory_space=pltpu.VMEM)] * 5,
         out_specs=(pl.BlockSpec(memory_space=pltpu.HBM), pl.BlockSpec(memory_space=pltpu.HBM)),
         scratch_shapes=[
             pltpu.VMEM(SHAPE, F32),
@@ -440,7 +444,7 @@
             pltpu.SemaphoreType.DMA((2, 8)),
         ],
         compiler_params=pltpu.CompilerParams(vmem_limit_bytes=32 * 1024 * 1024),
-    )(*handed, side_type)
+    )(*handed)
     full = (5, 4, 4, 4, 8, 256)
     return adv.reshape(full), new.reshape(full)
 

time: 14.3 us -> 14.1 us (0.986)
  Pallas kernels: 13.6 us -> 13.4 us
    pallas_call x1, Pallas kernels: 3.25 us -> 3.05 us  [per_device(): pl.pallas_call(surface_kernel, name='surface', out_shape=(jax.ShapeDtypeS...]
where the time goes in v9:
time: 14.1 us; the launch traced here: 14 us
  Pallas kernels  13.4 us (95%)
  between operations  0.64 us (5%)
    pallas_call x1, Pallas kernels, per_device(): pl.pallas_call(exchange_kernel, name='exchange', out_shape=(pltpu.VMEM(SH...  10.3 us
    pallas_call x1, Pallas kernels, per_device(): pl.pallas_call(surface_kernel, name='surface', out_shape=(jax.ShapeDtypeS...  3.05 us

profile of v9, /device:TPU:102, one launch (start us, length us, event | category | flops | bytes accessed | tf_op | source)
XLA Modules:
  0.0 14.0 jit_solution(12444493922787981121)
XLA Ops:
  0.6 10.3 %exchange.1 = (f32[5,4,4,32,256]{4,3,2,1,0:T(8,128)S(1)}, f32[5,4,4,32,256]{4,3,2,1,0:T(8,128)S(1)}, f32[4,5,4,32,256]{4,3,2,1,0:T(8,128)S(1)}, f32[2,80,256]{2,1,0:T(8,128)S(1)}, f32[5,4,4,32,256]{4,3,2,1,0:T(8,128)S(1)}) custom-call(f32[5,4,4,32,256]{4,3,2,1,0:T(8,128)} %bitcast.4, f32[5,4,4,32,256]{4,3,2,1,0:T(8,128)} %bitcast.5, s32[4,256]{1,0:T(4,128)} %nb_in.1, ...), custom_call_target="tpu_custom_call" | custom-call | tf_op jit(solution)/shard_map/exchange/pallas_call | solution.py:400
  11.0 3.0 %surface.1 = (f32[5,4,4,32,256]{4,3,2,1,0:T(8,128)}, f32[5,4,4,32,256]{4,3,2,1,0:T(8,128)}) custom-call(f32[5,4,4,32,256]{4,3,2,1,0:T(8,128)S(1)} %get-tuple-element.9.cv, f32[5,4,4,32,256]{4,3,2,1,0:T(8,128)S(1)} %get-tuple-element.10.acc, f32[4,5,4,32,256]{4,3,2,1,0:T(8,128)S(1)} %get-tuple-element.11.ghost, f32[2,80,256]{2,1,0:T(8,128)S(1)} %get-tuple-element.12.vert, ...), custom_call_target="tpu_custom_call" | custom-call | tf_op jit(solution)/shard_map/surface/pallas_call | solution.py:435

commit v10 on v9

--- a/solution.py
+++ b/solution.py
@@ -87,6 +87,23 @@
     return r, pressure, square * lax.rsqrt(square)
 
 
+def face_change(inner, outer, direction, sign, inner_known=None):
+    if inner_known is None:
+        r_in, p_in, c_in = primitive(inner)
+        v_in = inner[1 + direction] * r_in
+    else:
+        v_in, p_in, c_in = inner_known
+    r_out, p_out, c_out = primitive(outer)
+    v_out = outer[1 + direction] * r_out
+    lam = LIFT * jnp.maximum(jnp.abs(v_in) + c_in, jnp.abs(v_out) + c_out)
+    s_in, s_out = (sign * LIFT) * v_in, (sign * LIFT) * v_out
+    w_in, w_out = lam - s_in, lam - s_out
+    change = [w_out * outer[v] - w_in * inner[v] for v in range(5)]
+    change[1 + direction] = change[1 + direction] - (sign * LIFT) * (p_out - p_in)
+    change[4] = change[4] - (p_out * s_out - p_in * s_in)
+    return change
+
+
 def gather_slots(stage, side, lane_z):
     total = stage[side, pl.ds(0, 80, stride=8), :]
     for z in range(1, 8):
@@ -191,7 +208,9 @@
         pl.semaphore_wait(barrier, partners)
         launch(slice(4, 6))
 
-    first = layer == layers // 2 - 1
+    late = along == tiles // 2 - 1
+    first = jnp.logical_and(layer == layers // 2 - 1, jnp.logical_not(late))
+    second = jnp.logical_not(jnp.logical_or(first, late))
     pl.when(first)(open_vertical)
 
     for side in range(4):
@@ -200,8 +219,12 @@
         stage[side] = dot_nt(hi, send) + dot_nt(lo, send)
         packed[side ^ 1] = gather_slots(stage, side, lane_z)
 
-    pl.when(jnp.logical_not(first))(open_vertical)
-    launch(slice(0, 4))
+    pl.when(second)(open_vertical)
+
+    @pl.when(jnp.logical_not(late))
+    def _():
+        launch(slice(0, 4))
+
 
     def z_lines(line, carry):
         i, j = line // 4, line % 4
@@ -231,6 +254,11 @@
 
     lax.fori_loop(0, 16, z_lines, 0, unroll=4)
 
+    @pl.when(late)
+    def _():
+        open_vertical()
+        launch(slice(0, 4))
+
 
     def lines(direction, line, carry):
         a, k = line // 4, line % 4
@@ -302,6 +330,23 @@
             outer = jnp.where(kind == 0, got[part], jnp.where(kind == 2, FREE_STREAM[v], inner))
             ghost[side, v] = outer.reshape(4, 32, 256)
 
+    for side in (0, 1):
+        face, sign = 3 * side, 2.0 * side - 1.0
+
+        def x_face(node, carry):
+            a, b = node // 4, node % 4
+            rows_b = pl.ds(pl.multiple_of(8 * b, 8), 8)
+            at = (face, a, rows_b, slice(None))
+            q = [cv[(v,) + at] for v in range(5)]
+            outer = [ghost[side, v, a, rows_b, :] for v in range(5)]
+            known = prim[(0,) + at], prim[(3,) + at], prim[(4,) + at]
+            change = face_change(q, outer, 0, sign, known)
+            for v in range(5):
+                acc[(v,) + at] = acc[(v,) + at] + change[v]
+            return carry
+
+        lax.fori_loop(0, 16, x_face, 0, unroll=4)
+
     for way in (0, 1):
         _, there, comes = sends[4 + way]
 
@@ -337,8 +382,6 @@
                     q = [cv[v, i, j, rows_k, lanes] for v in range(5)]
                     total = [acc[v, i, j, rows_k, lanes] for v in range(5)]
                     faces = []
-                    if i in (0, 3):
-                        faces.append((0, 0 if i == 0 else 1, (j, k)))
                     if j in (0, 3):
                         faces.append((1, 2 if j == 0 else 3, (i, k)))
                     if k in (0, 3):

time: 14.1 us -> 14.5 us (1.028)
  Pallas kernels: 13.4 us -> 13.7 us
    pallas_call x1, Pallas kernels: 10.3 us -> 11.1 us  [per_device(): pl.pallas_call(exchange_kernel, name='exchange', out_shape=(pltpu.VMEM(SH...]
    pallas_call x1, Pallas kernels: 3.05 us -> 2.66 us  [per_device(): pl.pallas_call(surface_kernel, name='surface', out_shape=(jax.ShapeDtypeS...]
where the time goes in v10:
time: 14.5 us; the launch traced here: 14.4 us
  Pallas kernels  13.7 us (94%)
  between operations  0.64 us (4%)
    pallas_call x1, Pallas kernels, per_device(): pl.pallas_call(exchange_kernel, name='exchange', out_shape=(pltpu.VMEM(SH...  11.1 us
    pallas_call x1, Pallas kernels, per_device(): pl.pallas_call(surface_kernel, name='surface', out_shape=(jax.ShapeDtypeS...  2.66 us

profile of v10, /device:TPU:102, one launch (start us, length us, event | category | flops | bytes accessed | tf_op | source)
XLA Modules:
  0.0 14.4 jit_solution(10664789163332324232)
XLA Ops:
  0.6 11.1 %exchange.1 = (f32[5,4,4,32,256]{4,3,2,1,0:T(8,128)S(1)}, f32[5,4,4,32,256]{4,3,2,1,0:T(8,128)S(1)}, f32[4,5,4,32,256]{4,3,2,1,0:T(8,128)S(1)}, f32[2,80,256]{2,1,0:T(8,128)S(1)}, f32[5,4,4,32,256]{4,3,2,1,0:T(8,128)S(1)}) custom-call(f32[5,4,4,32,256]{4,3,2,1,0:T(8,128)} %bitcast.4, f32[5,4,4,32,256]{4,3,2,1,0:T(8,128)} %bitcast.5, s32[4,256]{1,0:T(4,128)} %nb_in.1, ...), custom_call_target="tpu_custom_call" | custom-call | tf_op jit(solution)/shard_map/exchange/pallas_call | solution.py:443
  11.7 2.7 %surface.1 = (f32[5,4,4,32,256]{4,3,2,1,0:T(8,128)}, f32[5,4,4,32,256]{4,3,2,1,0:T(8,128)}) custom-call(f32[5,4,4,32,256]{4,3,2,1,0:T(8,128)S(1)} %get-tuple-element.9.cv, f32[5,4,4,32,256]{4,3,2,1,0:T(8,128)S(1)} %get-tuple-element.10.acc, f32[4,5,4,32,256]{4,3,2,1,0:T(8,128)S(1)} %get-tuple-element.11.ghost, f32[2,80,256]{2,1,0:T(8,128)S(1)} %get-tuple-element.12.vert, ...), custom_call_target="tpu_custom_call" | custom-call | tf_op jit(solution)/shard_map/surface/pallas_call | solution.py:478

commit v11 on v10

--- a/solution.py
+++ b/solution.py
@@ -210,7 +210,6 @@
 
     late = along == tiles // 2 - 1
     first = jnp.logical_and(layer == layers // 2 - 1, jnp.logical_not(late))
-    second = jnp.logical_not(jnp.logical_or(first, late))
     pl.when(first)(open_vertical)
 
     for side in range(4):
@@ -219,11 +218,8 @@
         stage[side] = dot_nt(hi, send) + dot_nt(lo, send)
         packed[side ^ 1] = gather_slots(stage, side, lane_z)
 
-    pl.when(second)(open_vertical)
-
-    @pl.when(jnp.logical_not(late))
-    def _():
-        launch(slice(0, 4))
+    pl.when(jnp.logical_not(first))(open_vertical)
+    launch(slice(0, 4))
 
 
     def z_lines(line, carry):
@@ -253,11 +249,6 @@
         return carry
 
     lax.fori_loop(0, 16, z_lines, 0, unroll=4)
-
-    @pl.when(late)
-    def _():
-        open_vertical()
-        launch(slice(0, 4))
 
 
     def lines(direction, line, carry):

time: 14.5 us -> 14.5 us (level)
  no operation moved by 1% of the time
where the time goes in v11:
time: 14.5 us; the launch traced here: 14.4 us
  Pallas kernels  13.7 us (94%)
  between operations  0.64 us (4%)
    pallas_call x1, Pallas kernels, per_device(): pl.pallas_call(exchange_kernel, name='exchange', out_shape=(pltpu.VMEM(SH...  11.1 us
    pallas_call x1, Pallas kernels, per_device(): pl.pallas_call(surface_kernel, name='surface', out_shape=(jax.ShapeDtypeS...  2.66 us

profile of v11, /device:TPU:102, one launch (start us, length us, event | category | flops | bytes accessed | tf_op | source)
XLA Modules:
  0.0 14.4 jit_solution(7728027769787137984)
XLA Ops:
  0.6 11.1 %exchange.1 = (f32[5,4,4,32,256]{4,3,2,1,0:T(8,128)S(1)}, f32[5,4,4,32,256]{4,3,2,1,0:T(8,128)S(1)}, f32[4,5,4,32,256]{4,3,2,1,0:T(8,128)S(1)}, f32[2,80,256]{2,1,0:T(8,128)S(1)}, f32[5,4,4,32,256]{4,3,2,1,0:T(8,128)S(1)}) custom-call(f32[5,4,4,32,256]{4,3,2,1,0:T(8,128)} %bitcast.4, f32[5,4,4,32,256]{4,3,2,1,0:T(8,128)} %bitcast.5, s32[4,256]{1,0:T(4,128)} %nb_in.1, ...), custom_call_target="tpu_custom_call" | custom-call | tf_op jit(solution)/shard_map/exchange/pallas_call | solution.py:434
  11.7 2.7 %surface.1 = (f32[5,4,4,32,256]{4,3,2,1,0:T(8,128)}, f32[5,4,4,32,256]{4,3,2,1,0:T(8,128)}) custom-call(f32[5,4,4,32,256]{4,3,2,1,0:T(8,128)S(1)} %get-tuple-element.9.cv, f32[5,4,4,32,256]{4,3,2,1,0:T(8,128)S(1)} %get-tuple-element.10.acc, f32[4,5,4,32,256]{4,3,2,1,0:T(8,128)S(1)} %get-tuple-element.11.ghost, f32[2,80,256]{2,1,0:T(8,128)S(1)} %get-tuple-element.12.vert, ...), custom_call_target="tpu_custom_call" | custom-call | tf_op jit(solution)/shard_map/surface/pallas_call | solution.py:469

commit v12 on v9

--- a/solution.py
+++ b/solution.py
@@ -187,12 +187,13 @@
     loads[2].wait()
     reg_load.start()
 
-    def open_vertical():
+    def open_vertical(order=(4, 5)):
         pl.semaphore_wait(barrier, partners)
-        launch(slice(4, 6))
+        for n in order:
+            launch(slice(n, n + 1))
 
     first = layer == layers // 2 - 1
-    pl.when(first)(open_vertical)
+    pl.when(first)(functools.partial(open_vertical, (5, 4)))
 
     for side in range(4):
         hi, lo = split(trace_of(cv, side))

time: 14.1 us -> 14.1 us (level)
  no operation moved by 1% of the time
where the time goes in v12:
time: 14.1 us; the launch traced here: 14 us
  Pallas kernels  13.4 us (95%)
  between operations  0.64 us (5%)
    pallas_call x1, Pallas kernels, per_device(): pl.pallas_call(exchange_kernel, name='exchange', out_shape=(pltpu.VMEM(SH...  10.3 us
    pallas_call x1, Pallas kernels, per_device(): pl.pallas_call(surface_kernel, name='surface', out_shape=(jax.ShapeDtypeS...  3.05 us

profile of v12, /device:TPU:102, one launch (start us, length us, event | category | flops | bytes accessed | tf_op | source)
XLA Modules:
  0.0 14.0 jit_solution(2125657899823567762)
XLA Ops:
  0.6 10.3 %exchange.1 = (f32[5,4,4,32,256]{4,3,2,1,0:T(8,128)S(1)}, f32[5,4,4,32,256]{4,3,2,1,0:T(8,128)S(1)}, f32[4,5,4,32,256]{4,3,2,1,0:T(8,128)S(1)}, f32[2,80,256]{2,1,0:T(8,128)S(1)}, f32[5,4,4,32,256]{4,3,2,1,0:T(8,128)S(1)}) custom-call(f32[5,4,4,32,256]{4,3,2,1,0:T(8,128)} %bitcast.4, f32[5,4,4,32,256]{4,3,2,1,0:T(8,128)} %bitcast.5, s32[4,256]{1,0:T(4,128)} %nb_in.1, ...), custom_call_target="tpu_custom_call" | custom-call | tf_op jit(solution)/shard_map/exchange/pallas_call | solution.py:401
  11.0 3.0 %surface.1 = (f32[5,4,4,32,256]{4,3,2,1,0:T(8,128)}, f32[5,4,4,32,256]{4,3,2,1,0:T(8,128)}) custom-call(f32[5,4,4,32,256]{4,3,2,1,0:T(8,128)S(1)} %get-tuple-element.9.cv, f32[5,4,4,32,256]{4,3,2,1,0:T(8,128)S(1)} %get-tuple-element.10.acc, f32[4,5,4,32,256]{4,3,2,1,0:T(8,128)S(1)} %get-tuple-element.11.ghost, f32[2,80,256]{2,1,0:T(8,128)S(1)} %get-tuple-element.12.vert, ...), custom_call_target="tpu_custom_call" | custom-call | tf_op jit(solution)/shard_map/surface/pallas_call | solution.py:436
